TPU v7x, 32 devices: a whole 2x2x4 slice. The times are simulated.
32 devices in a mesh: seq: 16 (over z, y, x), head: 2 (over core).
Axes of the slice: x: 2, y: 2, z: 4, core: 2. Of those that a mesh axis runs over, the one named last changes fastest.
Arguments:
- inner_acts: bfloat16 [4096, 8192], P('seq', 'head'), may hold values from -0.4375 to 0.4375
- out_grad: bfloat16 [4096, 8192], P('seq', 'head'), may hold values from -0.4375 to 0.4375
- write_proj: bfloat16 [4096, 128], P('seq'), may hold values from -3 to 3
- read_proj: bfloat16 [4096, 128], P('seq'), may hold values from -3 to 3
- log_decay: float32 [4096, 64], P('seq', 'head'), may hold values from -2.5 to 0, as said below
- w_in: bfloat16 [4096, 8192], P('seq', 'head'), may hold values from -0.09375 to 0.09375
Outputs:
- input_grad: bfloat16 [4096, 4096], P('seq', 'head')
- act_grad: bfloat16 [4096, 8192], P('seq', 'head')
- write_grad: float32 [4096, 128], P('seq')
- read_grad: float32 [4096, 128], P('seq')
Inputs may be any that keep to these rules, and one draw needn't show every extreme that they name: `log_decay`: natural log of a decay factor of each head at each token; every entry is negative.
All inputs are finite; a program needn't handle non-finite values.
Results may differ from a plain program's by a relative error of at most 0.019.
Values may be sent and summed in bfloat16 or wider, within the bound.
No kernel may reach another device: no remote copies, remote signals or barrier semaphores. Data moves between devices by JAX's collectives and lax.ppermute only.
A program may use at most 192 MiB of HBM per device.

v0:
```python
import functools

import jax
import jax.numpy as jnp
from jax import lax
from jax.experimental import pallas as pl
from jax.experimental.pallas import tpu as pltpu
from jax.sharding import PartitionSpec as P

RING = 4
LANES = 128
EXTRA = 16
NT = (((1,), (1,)), ((), ()))
TN = (((0,), (0,)), ((), ()))
NN = (((1,), (0,)), ((), ()))
bf16, f32 = jnp.bfloat16, jnp.float32


def mm(a, b, dims):
    return lax.dot_general(a, b, dims, preferred_element_type=f32)


def mm_exact(a, b, dims):
    return lax.dot_general(a, b, dims, precision=lax.Precision.HIGHEST, preferred_element_type=f32)


def spread(columns, width):
    rows = columns.shape[0]
    return jnp.concatenate(
        [jnp.broadcast_to(columns[:, h : h + 1], (rows, width)) for h in range(columns.shape[1])],
        axis=1,
    )


def iota(shape, axis):
    return lax.broadcasted_iota(jnp.int32, shape, axis)


def three_parts(value):
    first = value.astype(bf16).astype(f32)
    second = (value - first).astype(bf16).astype(f32)
    return first, second, value - first - second


def cumulate(n_heads, log_tiles, cum, cum_t):
    parts = jnp.concatenate([tile[...] for tile in log_tiles], axis=0)
    rows = parts.shape[0]
    source, head = iota((LANES, LANES), 0), iota((LANES, LANES), 1)
    pick = (source < 3 * n_heads) & (lax.rem(source, n_heads) == head)
    logs = mm(parts, pick.astype(f32).astype(bf16), NN)
    upto = (iota((rows, rows), 0) <= iota((rows, rows), 1)).astype(f32)
    cum[...] = mm_exact(upto, logs, TN)
    if cum_t is not None:
        cum_t[...] = mm_exact(logs, upto, TN)


def group_of(value, g, heads, axis):
    shift = lax.rem(LANES - g * heads, LANES)
    value = pltpu.roll(value, shift, axis)
    return value[:, :heads] if axis == 1 else value[:heads]


def diagonal(heads, half, lo, col, row, each):
    later = iota((half, half), 1) >= iota((half, half), 0)
    for h in range(heads):
        log = row[h : h + 1, lo : lo + half] - col[lo : lo + half, h : h + 1]
        each(h, jnp.exp(jnp.where(later, log, -jnp.inf)))


def cumulate_own(log_t, cum, cum_t):
    n_heads, rows = log_t.shape
    logs = jnp.concatenate([log_t[...], jnp.zeros((LANES - n_heads, rows), f32)], axis=0)
    upto = (iota((rows, rows), 0) <= iota((rows, rows), 1)).astype(f32)
    cum[...] = mm_exact(upto, logs, (((0,), (1,)), ((), ())))
    if cum_t is not None:
        cum_t[...] = mm_exact(logs, upto, NN)


def edge_kernel(n_heads, at, x, dy, b, c, log_t, *refs):
    messages, cum = refs[:RING], refs[RING]
    g = pl.program_id(0)
    heads = n_heads // RING
    rows = x.shape[0]
    width = x.shape[1] // heads
    n = b.shape[1]

    @pl.when(g == 0)
    def _():
        cumulate_own(log_t, cum, None)

    col = group_of(cum[...], g, heads, 1)
    last = col[rows - 1 : rows, :]
    tailed = (x[...].astype(f32) * spread(jnp.exp(last - col), width)).astype(bf16)
    decayed = (dy[...].astype(f32) * spread(jnp.exp(col), width)).astype(bf16)
    ends = mm(b[...], tailed, TN).astype(bf16)
    fronts = mm(c[...], decayed, TN).astype(bf16)
    log = spread(last, width)
    for j in range(RING):

        @pl.when(lax.bitwise_xor(at[0], g) == j)
        def _():
            messages[j][:n] = ends
            messages[j][n : 2 * n] = fronts
            write_log(messages[j], log)


def pack_kernel(n_heads, dy, b, c, log_t, out):
    rows, columns = dy.shape
    fill = jnp.zeros((LANES - 3 * n_heads, rows), f32)
    logs = jnp.concatenate([*three_parts(log_t[...]), fill], axis=0)
    out[:, :columns] = dy[...]
    out[:, columns : columns + LANES] = b[...]
    out[:, columns + LANES : columns + 2 * LANES] = c[...]
    out[:, columns + 2 * LANES :] = logs.T.astype(bf16)


def own_kernel(n_heads, x, dy, b, c, log_t, write_local, read_local, total, cum, cum_t):
    g = pl.program_id(0)
    heads = n_heads // RING
    rows = x.shape[0]
    half = rows // 2
    width = x.shape[1] // heads

    @pl.when(g == 0)
    def _():
        total[...] = jnp.zeros_like(total)
        cumulate_own(log_t, cum, cum_t)

    col, row = group_of(cum[...], g, heads, 1), group_of(cum_t[...], g, heads, 0)
    mid = col[half - 1 : half, :]
    for i in range(2):
        lo = i * half
        parts = []

        def add(h, decay):
            span = slice(h * width, (h + 1) * width)
            parts.append(decay * mm(x[lo : lo + half, span], dy[lo : lo + half, span], NT))

        diagonal(heads, half, lo, col, row, add)
        total[lo : lo + half, lo : lo + half] += sum(parts)
    early = (x[:half].astype(f32) * spread(jnp.exp(mid - col[:half]), width)).astype(bf16)
    late = (dy[half:].astype(f32) * spread(jnp.exp(col[half:] - mid), width)).astype(bf16)
    total[:half, half:] += mm(early, late, NT)

    @pl.when(g == pl.num_programs(0) - 1)
    def _():
        write_local[...] = mm_exact(total[...], c[...].astype(f32), NN)
        read_local[...] = mm_exact(total[...], b[...].astype(f32), TN)


def block_kernel(n_heads, top, bottom, *refs):
    tiles, (act, fronts, log_row, cum_out, cum_t) = refs[:6], refs[6:]
    b = jnp.concatenate([tiles[0][...], tiles[1][...]], axis=0)
    c = jnp.concatenate([tiles[2][...], tiles[3][...]], axis=0)
    g = pl.program_id(0)
    heads = n_heads // RING
    half = top.shape[0]
    rows = 2 * half
    width = top.shape[1] // heads

    @pl.when(g == 0)
    def _():
        cumulate(n_heads, tiles[4:], cum_out, cum_t)

    col, row = group_of(cum_out[...], g, heads, 1), group_of(cum_t[...], g, heads, 0)
    mid, last = col[half - 1 : half, :], col[rows - 1 : rows, :]
    log_row[...] = spread(last, width)
    scores = mm(b, c, NT)
    late_f = bottom[...].astype(f32) * spread(jnp.exp(col[half:] - mid), width)
    late = late_f.astype(bf16)
    first = (top[...].astype(f32) * spread(jnp.exp(col[:half]), width)).astype(bf16)
    second = (late_f * spread(jnp.exp(mid), width)).astype(bf16)
    fronts[0] = (mm(c[:half], first, TN) + mm(c[half:], second, TN)).astype(bf16)
    cross = mm(scores[:half, half:].astype(bf16), late, NN)
    to_mid = jnp.exp(mid - col[:half])
    for i, dy in enumerate((top, bottom)):
        lo = i * half
        score = scores[lo : lo + half, lo : lo + half]

        def put(h, decay):
            span = slice(h * width, (h + 1) * width)
            out = mm((decay * score).astype(bf16), dy[:, span], NN)
            if i == 0:
                out += cross[:, span] * to_mid[:, h : h + 1]
            act[lo : lo + half, span] = out.astype(act.dtype)

        diagonal(heads, half, lo, col, row, put)


def log_over(p, logs, wanted):
    total = jnp.zeros_like(logs[0])
    for k in range(RING):
        total += jnp.where(wanted(lax.bitwise_xor(p, k)), logs[k], 0.0)
    return total


def combine_kernel(at, *refs):
    parts, (state_out, grad_out) = refs[:RING], refs[RING:]
    n = state_out.shape[0] - EXTRA
    logs = [log_of(part) for part in parts]
    p = at[0]
    state, grad = 0.0, 0.0
    for j in range(RING):
        own = lax.bitwise_xor(p, j)
        state += parts[j][:n].astype(f32) * jnp.exp(log_over(p, logs, lambda k: k > own))
        grad += parts[j][n : 2 * n].astype(f32) * jnp.exp(log_over(p, logs, lambda k: k < own))
    for out, value in ((state_out, state), (grad_out, grad)):
        out[:n] = value.astype(bf16)
        write_log(out, sum(logs))


def write_log(out, log):
    n, width = out.shape
    row = iota((EXTRA, width), 0)
    rows = jnp.zeros((EXTRA, width), f32)
    for i, part in enumerate(three_parts(log)):
        rows = jnp.where(row == i, part, rows)
    out[n - EXTRA :] = rows.astype(bf16)


def log_of(message):
    n = message.shape[0] - EXTRA
    tail = message[n:].astype(f32)
    return tail[0:1] + tail[1:2] + tail[2:3]


def merge_kernel(*refs):
    for near, far, out in ((*refs[:2], refs[4]), (*refs[2:4], refs[5])):
        n = near.shape[0] - EXTRA
        log = log_of(near)
        out[:n] = (near[:n].astype(f32) + far[:n].astype(f32) * jnp.exp(log)).astype(bf16)
        write_log(out, log + log_of(far))


def merged(near, far, weight=1.0):
    n = near.shape[0] - EXTRA
    log = log_of(near)
    value = near[:n].astype(f32) + far[:n].astype(f32) * (jnp.exp(log) * weight)
    return value, log + log_of(far)


def across_kernel(outer, at, state, state_far, grad, grad_far, out):
    n = out.shape[0] - EXTRA
    lower = at[1] < outer // 2
    (state_value, state_log), (grad_value, grad_log) = merged(state, state_far), merged(grad, grad_far)
    out[:n] = jnp.where(lower, state_value, grad_value).astype(bf16)
    write_log(out, jnp.where(lower, state_log, grad_log))


def settle_kernel(outer, at, state, grad, got, state_out, grad_out):
    lower = (at[1] < outer // 2).astype(f32)
    for near, weight, out in ((state, 1.0 - lower, state_out), (grad, lower, grad_out)):
        n = near.shape[0] - EXTRA
        value, log = merged(near, got, weight)
        out[:n] = value.astype(bf16)
        write_log(out, log)


def finish_kernel(n_heads, n_w, outer, share, at, *refs):
    locals_, refs = refs[:RING], refs[RING:]
    fronts, refs = refs[:RING], refs[RING:]
    quarters, refs = refs[:RING], refs[RING:]
    logs, refs = [r[...] for r in refs[:RING]], refs[RING:]
    tops, refs = refs[:RING], refs[RING:]
    bottoms, refs = refs[:RING], refs[RING:]
    cums, refs = refs[:RING], refs[RING:]
    w, refs = refs[:n_w], refs[n_w:]
    x, acts, own, write, *tiles, total = refs
    g, p = pl.program_id(0), at[0]
    heads = n_heads // RING
    rows = own.shape[0]
    width = own.shape[1] // heads
    n = quarters[0].shape[0] - EXTRA
    source = lax.bitwise_xor(p, g)
    carried = quarters[0][:n].astype(f32)
    for j in range(1, RING):
        carried = jnp.where(source == j, quarters[j][:n].astype(f32), carried)

    @pl.when(g == 0)
    def _():
        write[...] = jnp.zeros_like(write)
        total[...] = jnp.zeros_like(total)

    added = [front[0].astype(f32) for front in fronts]
    for j in range(RING):
        col = group_of(cums[j][...], g, heads, 1)
        tail = spread(jnp.exp(col[rows - 1 : rows, :] - col), width)
        place = lax.bitwise_xor(p, j)
        grads = carried * jnp.exp(log_over(p, logs, lambda k: k > place))
        for i in range(RING):
            if i != j:
                there = lax.bitwise_xor(p, i)
                weight = jnp.exp(log_over(p, logs, lambda k: (k > place) & (k < there)))
                grads += added[i] * jnp.where(there > place, weight, 0.0)
        grads = grads.astype(bf16)
        b = jnp.concatenate([tops[j][...], bottoms[j][...]], axis=0)
        out = mm(b, grads, NN) * tail + locals_[j][...].astype(f32)
        out = out.astype(acts.dtype)
        acts[j * rows : (j + 1) * rows, :] = out
        if j == 0:
            own[...] = out
            write[...] += mm((x[...].astype(f32) * tail).astype(bf16), grads, NT)
    for k in range(n_w):
        n_rows = w[k].shape[0]
        total[:, k * n_rows : (k + 1) * n_rows] += mm(acts[...], w[k][...], NT)

    @pl.when(g == pl.num_programs(0) - 1)
    def _():
        if len(tiles) == 1:
            for k in range(n_w):
                put_tile(tiles[0], lax.rem(at[1] + k, outer), total, k, n_rows)
        else:
            for tile in tiles:
                tile[...] = jnp.zeros_like(tile)
            for k in range(n_w):
                o = lax.rem(at[1] + k, outer)
                for tile, side in zip(tiles, (at[2], 1 - at[2])):

                    @pl.when(lax.div(o, share) == side)
                    def _():
                        put_tile(tile, lax.rem(o, share), total, k, n_rows)


def put_tile(tile, slot, total, k, n_rows):
    rows = total.shape[0] // RING
    for j in range(RING):
        part = total[j * rows : (j + 1) * rows, k * n_rows : (k + 1) * n_rows]
        tile[j, slot] = part.astype(tile.dtype)


def read_kernel(n_heads, at, *refs):
    tops, refs = refs[:RING], refs[RING:]
    bottoms, refs = refs[:RING], refs[RING:]
    cums, refs = list(refs[: RING - 1]), refs[RING - 1 :]
    log_tiles, refs = refs[:2], refs[2:]
    parts, (carried, *outs, last_cum) = refs[:RING], refs[RING:]
    cumulate(n_heads, log_tiles, last_cum, None)
    cums.append(last_cum)
    logs = [log_of(part) for part in parts]
    p = at[0]
    heads = n_heads // RING
    half = tops[0].shape[0]
    n = carried.shape[0] - EXTRA
    width = carried.shape[1] // heads
    for j in range(RING):
        own = lax.bitwise_xor(p, j)
        total = carried[:n].astype(f32) * jnp.exp(log_over(p, logs, lambda k: k < own))
        for i in range(RING):
            if i != j:
                there = lax.bitwise_xor(p, i)
                weight = jnp.exp(log_over(p, logs, lambda k: (k < own) & (k > there)))
                total += parts[i][:n].astype(f32) * jnp.where(there < own, weight, 0.0)
        states = total.astype(bf16)
        decay = spread(jnp.exp(group_of(cums[j][...], p, heads, 1)), width)
        for i, dy in enumerate((tops[j], bottoms[j])):
            at_rows = slice(i * half, (i + 1) * half)
            scaled = (dy[...].astype(f32) * decay[at_rows]).astype(bf16)
            outs[j][at_rows] = mm(scaled, states, NT).astype(bf16)


def place_kernel(outer, share, at, *refs):
    blocks, late, out = refs[:RING], refs[RING:-1], refs[-1]
    p, z, side = at[0], at[1], at[2]
    width = out.shape[1] // (share * RING)
    last = lax.rem(z + outer - 1, outer)
    for slot in range(share):
        for j in range(RING):
            column = pl.multiple_of((slot * RING + lax.bitwise_xor(p, j)) * width, width)

            @pl.when(side * share + slot == last)
            def _():
                out[:, pl.ds(column, width)] = late[j][...]

            @pl.when(side * share + slot != last)
            def _():
                out[:, pl.ds(column, width)] = blocks[j][slot]


def call(kernel, name, grid, in_specs, out_specs, out_shape, scratch=(), after=()):
    n_in, n_after = len(in_specs), len(after)

    def body(at, *refs):
        kernel(at, *refs[:n_in], *refs[n_in + n_after :])

    fn = pl.pallas_call(
        body,
        grid_spec=pltpu.PrefetchScalarGridSpec(
            num_scalar_prefetch=1,
            grid=grid,
            in_specs=list(in_specs) + [pl.BlockSpec(memory_space=pl.ANY)] * n_after,
            out_specs=out_specs,
            scratch_shapes=list(scratch),
        ),
        out_shape=out_shape,
        compiler_params=pltpu.CompilerParams(vmem_limit_bytes=56 * 2**20),
        cost_estimate=pl.CostEstimate(flops=0, bytes_accessed=0, transcendentals=0),
        name=name,
    )
    return lambda *operands: fn(*operands, *after)


def local(x, dy, write_proj, read_proj, log_decay, w_in):
    rows, columns = x.shape
    half = rows // 2
    state_dim = write_proj.shape[1]
    n_heads = log_decay.shape[1]
    heads = n_heads // RING
    width = columns // n_heads
    part = heads * width
    w_rows = w_in.shape[0]
    n_seq, n_head = lax.axis_size("seq"), lax.axis_size("head")
    outer = n_seq // RING
    place = lax.axis_index("seq")
    side = lax.axis_index("head")
    p, z = place % RING, place // RING
    at = jnp.stack([p, z, side]).astype(jnp.int32)

    def swap(value, j):
        return lax.ppermute(value, "seq", [(s, s ^ j) for s in range(n_seq)])

    def along(value, d):
        return lax.ppermute(
            value, "seq", [(s, s + d * RING) for s in range(n_seq) if 0 <= s + d * RING < n_seq]
        )

    w_blocks = [w_in]

    def turn_w():
        turn = [(s, (s - RING) % n_seq) for s in range(n_seq)]
        w_blocks.append(lax.ppermute(w_blocks[-1], "seq", turn))

    turn_w()

    def const(*shape):
        return pl.BlockSpec(shape, lambda g, q: (0,) * len(shape))

    by_group = pl.BlockSpec((rows, part), lambda g, q: (0, g))
    state_spec = pl.BlockSpec((1, state_dim, part), lambda g, q: (g, 0, 0))
    log_spec = pl.BlockSpec((1, part), lambda g, q: (0, g))
    cum_spec = const(rows, LANES)
    proj_spec = const(rows, state_dim)
    message_spec = const(state_dim + EXTRA, part)
    shape = jax.ShapeDtypeStruct
    state_shape = shape((RING, state_dim, part), bf16)
    log_shape = shape((1, columns), f32)
    cum_shape = shape((rows, LANES), f32)
    message_shape = shape((state_dim + EXTRA, part), bf16)
    cum_scratch, cum_t_scratch = pltpu.VMEM((rows, LANES), f32), pltpu.VMEM((LANES, rows), f32)

    log_in_spec = const(n_heads, rows)
    log_t = log_decay.T
    own_specs = [by_group, by_group, proj_spec, proj_spec, log_in_spec]
    part_spec = const(2 * state_dim + EXTRA, part)
    parts = call(
        functools.partial(edge_kernel, n_heads),
        "edges",
        (RING,),
        own_specs,
        [part_spec] * RING,
        [shape((2 * state_dim + EXTRA, part), bf16)] * RING,
        [cum_scratch],
    )(at, x, dy, write_proj, read_proj, log_t)
    parts = [parts[0]] + [swap(parts[j], j) for j in range(1, RING)]

    write_local, read_local = call(
        functools.partial(lambda *refs: own_kernel(n_heads, *refs[1:])),
        "own_tokens",
        (RING,),
        own_specs,
        [proj_spec] * 2,
        [shape((rows, state_dim), f32)] * 2,
        [pltpu.VMEM((rows, rows), f32), cum_scratch, cum_t_scratch],
    )(at, x, dy, write_proj, read_proj, log_t)

    packed = call(
        functools.partial(lambda *refs: pack_kernel(n_heads, *refs[1:])),
        "pack",
        (1,),
        [const(rows, columns), proj_spec, proj_spec, log_in_spec],
        const(rows, columns + 3 * LANES),
        shape((rows, columns + 3 * LANES), bf16),
    )(at, dy, write_proj, read_proj, log_t)

    def halves(width, column):
        upper = pl.BlockSpec((half, width), lambda g, q: (0, column(g, q)))
        lower = pl.BlockSpec((half, width), lambda g, q: (1, column(g, q)))
        return [(upper, lower)] * (RING - 1) + [(upper, upper)]

    half_specs = halves(part, lambda g, q: g)
    mine_specs = halves(part, lambda g, q: q[0])
    tile_specs = [halves(LANES, lambda g, q, i=i: columns // LANES + i) for i in range(3)]

    def block(j, top, bottom, after=()):
        return call(
            functools.partial(lambda *refs: block_kernel(n_heads, *refs[1:])),
            "tokens",
            (RING,),
            [*half_specs[j]] + [spec for specs in tile_specs for spec in specs[j]],
            [by_group, state_spec, log_spec, cum_spec],
            [shape((rows, columns), bf16), state_shape, log_shape, cum_shape],
            [cum_t_scratch],
            after,
        )(at, top, bottom, *([top, bottom] * 3))

    results = [block(0, packed, packed)]
    logs = [results[0][2]]
    packed, parts, logs, read_local = lax.optimization_barrier((packed, parts, logs, read_local))
    from_x, from_y = lax.optimization_barrier((swap(packed, 1), swap(packed, 2)))

    def combine():
        return call(
            combine_kernel,
            "messages",
            (1,),
            [part_spec] * RING,
            [message_spec] * 2,
            [message_shape] * 2,
        )(at, *parts)

    def merge(*pairs):
        return call(
            lambda q, *refs: merge_kernel(*refs),
            "merge",
            (1,),
            [message_spec] * 4,
            [message_spec] * 2,
            [message_shape] * 2,
        )(at, *pairs)

    state_span, grad_span = combine()
    d = 1
    while d < outer:
        if outer == 4 and d == 2:
            got = lax.ppermute(across, "seq", [(s, s ^ (d * RING)) for s in range(n_seq)])
            state_part, grad_part = call(
                functools.partial(settle_kernel, outer),
                "settle",
                (1,),
                [message_spec] * 3,
                [message_spec] * 2,
                [message_shape] * 2,
            )(at, state_part, grad_part, got)
            got, w_blocks[-1] = lax.optimization_barrier((got, w_blocks[-1]))
            break
        state_got, grad_got = along(state_span, d), along(grad_span, -d)
        if d == 1:
            state_part, grad_part = state_got, grad_got
        else:
            state_part, grad_part = merge(state_part, state_got, grad_part, grad_got)
        if outer == 4:
            across = call(
                functools.partial(across_kernel, outer),
                "across",
                (1,),
                [message_spec] * 4,
                message_spec,
                message_shape,
            )(at, state_span, state_got, grad_span, grad_got)
        elif 2 * d < outer:
            state_span, grad_span = merge(state_span, state_got, grad_span, grad_got)
        d *= 2
    turn_w()
    from_x, from_y, grad_part = lax.optimization_barrier((from_x, from_y, grad_part))
    blocks = [(packed, packed), (from_x, from_x), (from_y, from_y)]
    blocks.append((swap(from_x[:half], 2), swap(from_y[half:], 1)))
    results += [block(j, *blocks[j]) for j in range(1, RING - 1)]
    logs += [v[2] for v in results[1:]]
    logs, grad_part = lax.optimization_barrier((logs, grad_part))
    grad_parts = [grad_part] + [swap(grad_part, j) for j in range(1, RING)]

    read_parts = call(
        functools.partial(read_kernel, n_heads),
        "read_carry",
        (1,),
        [spec[0] for spec in mine_specs]
        + [spec[1] for spec in mine_specs]
        + [cum_spec] * (RING - 1)
        + list(tile_specs[2][-1])
        + [part_spec] * RING
        + [message_spec],
        [proj_spec] * RING,
        [shape((rows, state_dim), bf16)] * RING,
        [cum_scratch],
    )(
        at,
        *[top for top, _ in blocks],
        *[bottom for _, bottom in blocks],
        *[v[3] for v in results],
        *blocks[-1],
        *parts,
        state_part,
    )

    read_parts, w_blocks[-1] = lax.optimization_barrier((read_parts, w_blocks[-1]))
    after = [read_parts[0]]
    if outer > 2:
        after.append(w_blocks[-1])
    results.append(block(RING - 1, *blocks[-1], after))
    logs.append(results[-1][2])
    while len(w_blocks) < outer:
        turn_w()
    local_acts, fronts, _, cums = zip(*results)
    two = n_head == 2 and w_rows % LANES == 0
    share = outer // n_head
    n_w = outer - 1 if two else outer
    tall = pl.BlockSpec((RING * rows, part), lambda g, q: (0, g))
    w_spec = pl.BlockSpec((w_rows, part), lambda g, q: (0, g))
    tile_shapes = [(RING, share, rows, w_rows)] * 2 if two else [(RING, outer, rows, w_rows)]
    acts, act_grad, write_carry, *tiles = call(
        functools.partial(finish_kernel, n_heads, n_w, outer, share),
        "finish",
        (RING,),
        [by_group] * RING
        + [state_spec] * RING
        + [message_spec] * RING
        + [log_spec] * RING
        + [spec[0] for spec in tile_specs[0]]
        + [spec[1] for spec in tile_specs[0]]
        + [cum_spec] * RING
        + [w_spec] * n_w
        + [by_group],
        [tall, by_group, proj_spec] + [const(*v) for v in tile_shapes],
        [
            shape((RING * rows, columns), bf16),
            shape((rows, columns), bf16),
            shape((rows, state_dim), f32),
        ]
        + [shape(v, bf16) for v in tile_shapes],
        [pltpu.VMEM((RING * rows, n_w * w_rows), f32)],
    )(
        at,
        *local_acts,
        *fronts,
        *grad_parts,
        *logs,
        *[top for top, _ in blocks],
        *[bottom for _, bottom in blocks],
        *cums,
        *w_blocks[:n_w],
        x,
    )

    def to_owners(tile):
        return [tile[0]] + [swap(tile[j], j) for j in range(1, RING)]

    if two:
        mine, theirs = tiles
        got = lax.ppermute(theirs, "head", [(0, 1), (1, 0)])
        early = (mine.astype(f32) + got.astype(f32)).astype(bf16)
        read_got = [swap(read_parts[j], j) for j in range(1, RING)]
        early, read_got, w_last = lax.optimization_barrier((early, read_got, w_blocks[-1]))
        tile = mm(acts, w_last, NT).astype(bf16)

        def owner(s):
            return (s // RING + outer - 1) % outer // share

        both_axes = ("seq", "head")
        got = lax.ppermute(
            tile, both_axes, [(2 * s + 1 - owner(s), 2 * s + owner(s)) for s in range(n_seq)]
        )
        tile = (tile.astype(f32) + got.astype(f32)).astype(bf16).reshape(RING, rows, w_rows)
        late = [tile[0]] + [
            lax.ppermute(
                tile[j],
                both_axes,
                [(2 * s + owner(s), 2 * (s ^ j) + owner(s)) for s in range(n_seq)],
            )
            for j in range(1, RING)
        ]
        early = to_owners(early)
        input_grad = pl.pallas_call(
            functools.partial(place_kernel, outer, share),
            in_specs=[pl.BlockSpec(memory_space=pltpu.SMEM)]
            + [pl.BlockSpec(memory_space=pltpu.VMEM)] * (2 * RING),
            out_specs=pl.BlockSpec(memory_space=pltpu.VMEM),
            out_shape=shape((rows, share * RING * w_rows), bf16),
            compiler_params=pltpu.CompilerParams(vmem_limit_bytes=32 * 2**20),
            name="place",
        )(at, *early, *late)
    else:
        summed = lax.psum_scatter(tiles[0], "head", scatter_dimension=1, tiled=True)
        pieces = jnp.take(jnp.stack(to_owners(summed)), p ^ jnp.arange(RING), axis=0)
        input_grad = pieces.transpose(2, 1, 0, 3).reshape(rows, share * RING * w_rows)
    if not two:
        read_got = [swap(read_parts[j], j) for j in range(1, RING)]
    read_carry = read_parts[0].astype(f32) + sum(v.astype(f32) for v in read_got)
    both = jnp.stack([write_local + write_carry, read_local + read_carry])
    if n_head == 2:
        both = both + lax.ppermute(both, "head", [(0, 1), (1, 0)])
    else:
        both = lax.psum(both, "head")
    return (input_grad, act_grad, both[0], both[1])


def solution(mesh):
    return jax.shard_map(
        local,
        mesh=mesh,
        in_specs=(
            P("seq", "head"),
            P("seq", "head"),
            P("seq", None),
            P("seq", None),
            P("seq", "head"),
            P("seq", "head"),
        ),
        out_specs=(P("seq", "head"), P("seq", "head"), P("seq", None), P("seq", None)),
        check_vma=False,
    )
```

profile of v0, /device:TPU:1, one launch (start us, length us, event | category | flops | bytes accessed | tf_op | source)
XLA Modules:
  0.0 204.5 jit_solution(5654347854279396864)
XLA Ops:
  0.6 4.2 %collective-permute-start.10 = (bf16[256,4096]{1,0:T(8,128)(2,1)}, bf16[256,4096]{1,0:T(8,128)(2,1)}, u32[]{:S(2)}, u32[]{:S(2)}) collective-permute-start(bf16[256,4096]{1,0:T(8,128)(2,1)} %refs_28_.1), channel_id=1, source_target_pairs={{0,24},{2,26},{4,28},{6,30},{8,0},{10,2},{12,4},{14,6},{16,8},{18,... | collective-permute-start | bytes 6291464 | tf_op jit(solution)/shard_map/ppermute | solution.py:430
  5.4 8.1 %edges.1 = (bf16[272,1024]{1,0:T(8,128)(2,1)}, bf16[272,1024]{1,0:T(8,128)(2,1)}, bf16[272,1024]{1,0:T(8,128)(2,1)}, bf16[272,1024]{1,0:T(8,128)(2,1)}) custom-call(s32[3]{0:T(128)} %pad_add_fusion.at, bf16[256,4096]{1,0:T(8,128)(2,1)} %refs_31_.1, bf16[256,4096]{1,0:T(8,128)(2,1)} %refs_1_.5, bf16[256,128]{1,0:T(8,128)(2,1)} %refs_2_.5, ...), custom_call_target="tpu_custom_call" | custom-call | tf_op jit(solution)/shard_map/edges/pallas_call | solution.py:399
  16.2 3.8 %pack.1.refs_0_.refs_1_.refs_2_.refs_3_.refs_4_.refs_5_.refs_6_.refs_7_.refs_16_.refs_20_ = bf16[256,4480]{1,0:T(8,128)(2,1)} custom-call(s32[3]{0:T(128)} %pad_add_fusion.at, bf16[256,4096]{1,0:T(8,128)(2,1)} %refs_1_.5, bf16[256,128]{1,0:T(8,128)(2,1)} %refs_2_.5, bf16[256,128]{1,0:T(8,128)(2,1)} %refs_3_.3, f32[32,256]{1,0:T(8,128)} %bitcast.23), custom_call_target="tpu_custom_call" | custom-call | tf_op jit(solution)/shard_map/pack/pallas_call | solution.py:399
  20.0 8.2 %own_tokens.1 = (f32[256,128]{1,0:T(8,128)}, f32[256,128]{1,0:T(8,128)}) custom-call(s32[3]{0:T(128)} %pad_add_fusion.at, bf16[256,4096]{1,0:T(8,128)(2,1)} %refs_31_.1, bf16[256,4096]{1,0:T(8,128)(2,1)} %refs_1_.5, bf16[256,128]{1,0:T(8,128)(2,1)} %refs_2_.5, bf16[256,128]{1,0:T(8,128)(2,1)} %refs_3_.3, f32[32,256]{1,0:T(8,128)} %bitcast.24), custom_call_target="tpu_custom_call" | custom-call | tf_op jit(solution)/shard_map/own_tokens/pallas_call | solution.py:399
  28.2 8.1 %tokens.4 = (bf16[256,4096]{1,0:T(8,128)(2,1)}, bf16[4,128,1024]{2,1,0:T(8,128)(2,1)}, f32[1,4096]{1,0:T(1,128)}, f32[256,128]{1,0:T(8,128)}) custom-call(s32[3]{0:T(128)} %pad_add_fusion.at, bf16[256,4480]{1,0:T(8,128)(2,1)} %pack.1.refs_0_.refs_1_.refs_2_.refs_3_.refs_4_.refs_5_.refs_6_.refs_7_.refs_16_.refs_20_, ...), custom_call_target="tpu_custom_call" | custom-call | tf_op jit(solution)/shard_map/tokens/pallas_call | solution.py:399
  36.3 3.5 %collective-permute-done.2.refs_3_.refs_16_ = bf16[272,1024]{1,0:T(8,128)(2,1)S(1)} collective-permute-done((bf16[272,1024]{1,0:T(8,128)(2,1)}, bf16[272,1024]{1,0:T(8,128)(2,1)S(1)}, u32[]{:S(2)}, u32[]{:S(2)}) %collective-permute-start.2) | collective-permute-done | bytes 557088 | tf_op jit(solution)/shard_map/ppermute | solution.py:419
  42.1 3.4 %messages.1 = (bf16[144,1024]{1,0:T(8,128)(2,1)}, bf16[144,1024]{1,0:T(8,128)(2,1)}) custom-call(s32[3]{0:T(128)} %pad_add_fusion.at, bf16[272,1024]{1,0:T(8,128)(2,1)} %get-tuple-element.76.refs_0_.refs_13_, bf16[272,1024]{1,0:T(8,128)(2,1)} %copy-done.6, bf16[272,1024]{1,0:T(8,128)(2,1)} %copy-done.7, bf16[272,1024]{1,0:T(8,128)(2,1)} %copy-done.8), custom_call_target="tpu_custom_call" | custom-call | tf_op jit(solution)/shard_map/messages/pallas_call | solution.py:399
  48.2 7.6 %collective-permute-done.5.refs_1_.refs_0_ = bf16[144,1024]{1,0:T(8,128)(2,1)S(1)} collective-permute-done((bf16[144,1024]{1,0:T(8,128)(2,1)}, bf16[144,1024]{1,0:T(8,128)(2,1)S(1)}, u32[]{:S(2)}, u32[]{:S(2)}) %collective-permute-start.5) | collective-permute-done | bytes 294944 | tf_op jit(solution)/shard_map/ppermute | solution.py:422
  57.2 2.8 %across.1 = bf16[144,1024]{1,0:T(8,128)(2,1)} custom-call(s32[3]{0:T(128)} %pad_add_fusion.at, bf16[144,1024]{1,0:T(8,128)(2,1)} %get-tuple-element.80.refs_0_, bf16[144,1024]{1,0:T(8,128)(2,1)} %copy-done.9, bf16[144,1024]{1,0:T(8,128)(2,1)} %get-tuple-element.81.refs_2_, bf16[144,1024]{1,0:T(8,128)(2,1)} %copy-done.10), custom_call_target="tpu_custom_call" | custom-call | tf_op jit(solution)/shard_map/across/pallas_call | solution.py:399
  60.1 3.9 %collective-permute-start.7 = (bf16[144,1024]{1,0:T(8,128)(2,1)}, bf16[144,1024]{1,0:T(8,128)(2,1)S(1)}, u32[]{:S(2)}, u32[]{:S(2)}) collective-permute-start(bf16[144,1024]{1,0:T(8,128)(2,1)} %across.1), channel_id=1, source_target_pairs={{0,16},{2,18},{4,20},{6,22},{8,24},{10,26},{12,28},{14,30},{16,0},... | collective-permute-start | bytes 884744 | tf_op jit(solution)/shard_map/ppermute | solution.py:534
  64.0 13.4 %collective-permute-done.7.refs_2_ = bf16[144,1024]{1,0:T(8,128)(2,1)S(1)} collective-permute-done((bf16[144,1024]{1,0:T(8,128)(2,1)}, bf16[144,1024]{1,0:T(8,128)(2,1)S(1)}, u32[]{:S(2)}, u32[]{:S(2)}) %collective-permute-start.7) | collective-permute-done | bytes 294944 | tf_op jit(solution)/shard_map/ppermute | solution.py:534
  77.4 3.8 %collective-permute-start.11 = (bf16[256,4096]{1,0:T(8,128)(2,1)}, bf16[256,4096]{1,0:T(8,128)(2,1)}, u32[]{:S(2)}, u32[]{:S(2)}) collective-permute-start(bf16[256,4096]{1,0:T(8,128)(2,1)} %collective-permute-done.10.refs_29_), channel_id=1, source_target_pairs={{0,24},{2,26},{4,28},{6,30},{8,0},{10,2},{12,4},{14,6},{16,8},{18,... | collective-permute-start | bytes 6291464 | tf_op jit(solution)/shard_map/ppermute | solution.py:430
  81.2 2.7 %settle.1 = (bf16[144,1024]{1,0:T(8,128)(2,1)}, bf16[144,1024]{1,0:T(8,128)(2,1)}) custom-call(s32[3]{0:T(128)} %pad_add_fusion.at, bf16[144,1024]{1,0:T(8,128)(2,1)} %copy-done.9, bf16[144,1024]{1,0:T(8,128)(2,1)} %copy-done.10, bf16[144,1024]{1,0:T(8,128)(2,1)} %copy-done.15), custom_call_target="tpu_custom_call" | custom-call | tf_op jit(solution)/shard_map/settle/pallas_call | solution.py:399
  84.0 6.0 %collective-permute-done.3.refs_0_.refs_1_.refs_2_.refs_3_.refs_4_.refs_5_.refs_6_.refs_7_.refs_17_.refs_21_ = bf16[256,4480]{1,0:T(8,128)(2,1)S(1)} collective-permute-done((bf16[256,4480]{1,0:T(8,128)(2,1)S(1)}, bf16[256,4480]{1,0:T(8,128)(2,1)S(1)}, u32[]{:S(2)}, u32[]{:S(2)}) %collective-permute-start.3) | collective-permute-done | bytes 2293792 | tf_op jit(solution)/shard_map/ppermute | solution.py:419
  93.9 8.0 %tokens.6 = (bf16[256,4096]{1,0:T(8,128)(2,1)}, bf16[4,128,1024]{2,1,0:T(8,128)(2,1)}, f32[1,4096]{1,0:T(1,128)}, f32[256,128]{1,0:T(8,128)}) custom-call(s32[3]{0:T(128)} %pad_add_fusion.at, bf16[256,4480]{1,0:T(8,128)(2,1)} %copy-done.3, bf16[256,4480]{1,0:T(8,128)(2,1)} %copy-done.3, bf16[256,4480]{1,0:T(8,128)(2,1)} %copy-done.3, ...), custom_call_target="tpu_custom_call" | custom-call | tf_op jit(solution)/shard_map/tokens/pallas_call | solution.py:399
  101.9 8.0 %tokens.5 = (bf16[256,4096]{1,0:T(8,128)(2,1)}, bf16[4,128,1024]{2,1,0:T(8,128)(2,1)}, f32[1,4096]{1,0:T(1,128)}, f32[256,128]{1,0:T(8,128)}) custom-call(s32[3]{0:T(128)} %pad_add_fusion.at, bf16[256,4480]{1,0:T(8,128)(2,1)} %copy-done.2, bf16[256,4480]{1,0:T(8,128)(2,1)} %copy-done.2, bf16[256,4480]{1,0:T(8,128)(2,1)} %copy-done.2, ...), custom_call_target="tpu_custom_call" | custom-call | tf_op jit(solution)/shard_map/tokens/pallas_call | solution.py:399
  109.8 5.4 %collective-permute-done.8.refs_3_.refs_11_.refs_0_.refs_2_.refs_4_.refs_6_.refs_19_ = bf16[128,4480]{1,0:T(8,128)(2,1)S(1)} collective-permute-done((bf16[128,4480]{1,0:T(8,128)(2,1)S(1)}, bf16[128,4480]{1,0:T(8,128)(2,1)S(1)}, u32[]{:S(2)}, u32[]{:S(2)}) %collective-permute-start.8) | collective-permute-done | bytes 1146912 | tf_op jit(solution)/shard_map/ppermute | solution.py:419
  115.2 1.9 collective-permute-done.9.refs_7_.refs_12_.refs_1_.refs_3_.refs_5_.refs_23_
  118.1 6.3 %read_carry.1 = (bf16[256,128]{1,0:T(8,128)(2,1)}, bf16[256,128]{1,0:T(8,128)(2,1)}, bf16[256,128]{1,0:T(8,128)(2,1)}, bf16[256,128]{1,0:T(8,128)(2,1)}) custom-call(s32[3]{0:T(128)} %pad_add_fusion.at, bf16[256,4480]{1,0:T(8,128)(2,1)} %pack.1.refs_0_.refs_1_.refs_2_.refs_3_.refs_4_.refs_5_.refs_6_.refs_7_.refs_16_.refs_20_, bf16[256,4480]{1,0:T(8,128)(2,1)} %copy-done.2, ...), custom_call_target="tpu_custom_call" | custom-call | tf_op jit(solution)/shard_map/read_carry/pallas_call | solution.py:399
  126.0 4.0 %collective-permute-start.19 = (bf16[256,4096]{1,0:T(8,128)(2,1)}, bf16[256,4096]{1,0:T(8,128)(2,1)S(1)}, u32[]{:S(2)}, u32[]{:S(2)}) collective-permute-start(bf16[256,4096]{1,0:T(8,128)(2,1)} %collective-permute-done.11.refs_9_.refs_30_), channel_id=1, source_target_pairs={{0,24},{2,26},{4,28},{6,30},{8,0},{10,2},{12,4},{14,6},{16,8},{18,... | collective-permute-start | bytes 6291464 | tf_op jit(solution)/shard_map/ppermute | solution.py:430
  132.7 7.9 %tokens.7 = (bf16[256,4096]{1,0:T(8,128)(2,1)}, bf16[4,128,1024]{2,1,0:T(8,128)(2,1)}, f32[1,4096]{1,0:T(1,128)}, f32[256,128]{1,0:T(8,128)}) custom-call(s32[3]{0:T(128)} %pad_add_fusion.at, bf16[128,4480]{1,0:T(8,128)(2,1)} %copy-done.4, bf16[128,4480]{1,0:T(8,128)(2,1)} %copy-done.5, bf16[128,4480]{1,0:T(8,128)(2,1)} %copy-done.4, ...), custom_call_target="tpu_custom_call" | custom-call | tf_op jit(solution)/shard_map/tokens/pallas_call | solution.py:399
  140.6 3.7 %collective-permute-done.14.refs_11_ = bf16[144,1024]{1,0:T(8,128)(2,1)S(1)} collective-permute-done((bf16[144,1024]{1,0:T(8,128)(2,1)S(1)}, bf16[144,1024]{1,0:T(8,128)(2,1)S(1)}, u32[]{:S(2)}, u32[]{:S(2)}) %collective-permute-start.14) | collective-permute-done | bytes 294944 | tf_op jit(solution)/shard_map/ppermute | solution.py:419
  145.0 22.5 %finish.1 = (bf16[1024,4096]{1,0:T(8,128)(2,1)}, bf16[256,4096]{1,0:T(8,128)(2,1)}, f32[256,128]{1,0:T(8,128)}, bf16[4,2,256,256]{3,2,1,0:T(8,128)(2,1)}, bf16[4,2,256,256]{3,2,1,0:T(8,128)(2,1)}) custom-call(s32[3]{0:T(128)} %pad_add_fusion.at, bf16[256,4096]{1,0:T(8,128)(2,1)} %get-tuple-element.66.refs_0_, bf16[256,4096]{1,0:T(8,128)(2,1)} %get-tuple-element.84.refs_1_, ...), custom_call_target="tpu_custom_call" | custom-call | tf_op jit(solution)/shard_map/finish/pallas_call | solution.py:399
  167.5 2.9 %collective-permute-start.15 = (bf16[4,2,256,256]{3,2,1,0:T(8,128)(2,1)}, bf16[4,2,256,256]{3,2,1,0:T(8,128)(2,1)S(1)}, u32[]{:S(2)}, u32[]{:S(2)}) collective-permute-start(bf16[4,2,256,256]{3,2,1,0:T(8,128)(2,1)} %get-tuple-element.114), channel_id=1, source_target_pairs={{0,1},{1,0},{2,3},{3,2},{4,5},{5,4},{6,7},{7,6},{8,9},{9,8},{10,11... | collective-permute-start | bytes 3145736 | tf_op jit(solution)/shard_map/ppermute | solution.py:648
  176.0 5.8 %convolution_convert_fusion = bf16[1024,256]{1,0:T(8,128)(2,1)S(1)} fusion(bf16[1024,4096]{1,0:T(8,128)(2,1)} %get-tuple-element.119, bf16[256,4096]{1,0:T(8,128)(2,1)S(1)} %collective-permute-done.19), kind=kOutput, calls=%fused_computation.1 | convolution fusion | flops 2147745792 | bytes 11010048 | tf_op jit(solution)/shard_map/dot_general | solution.py:20
  183.2 1.9 collective-permute-start.27
  188.1 3.1 %collective-permute-start.24 = (bf16[256,256]{1,0:T(8,128)(2,1)S(1)}, bf16[256,256]{1,0:T(8,128)(2,1)S(1)}, u32[]{:S(2)}, u32[]{:S(2)}) collective-permute-start(bf16[256,256]{1,0:T(8,128)(2,1)S(1)} %get-tuple-element.134), channel_id=1, source_target_pairs={{1,3},{3,1},{5,7},{7,5},{8,10},{10,8},{12,14},{14,12},{16,18},{18,... | collective-permute-start | bytes 393224 | tf_op jit(solution)/shard_map/ppermute | solution.py:663
  191.2 2.1 %collective-permute-start.25 = (bf16[256,256]{1,0:T(8,128)(2,1)S(1)}, bf16[256,256]{1,0:T(8,128)(2,1)S(1)}, u32[]{:S(2)}, u32[]{:S(2)}) collective-permute-start(bf16[256,256]{1,0:T(8,128)(2,1)S(1)} %get-tuple-element.133), channel_id=1, source_target_pairs={{1,5},{3,7},{5,1},{7,3},{8,12},{10,14},{12,8},{14,10},{16,20},{18,... | collective-permute-start | bytes 393224 | tf_op jit(solution)/shard_map/ppermute | solution.py:663
  193.4 3.2 %collective-permute-start.26 = (bf16[256,256]{1,0:T(8,128)(2,1)S(1)}, bf16[256,256]{1,0:T(8,128)(2,1)S(1)}, u32[]{:S(2)}, u32[]{:S(2)}) collective-permute-start(bf16[256,256]{1,0:T(8,128)(2,1)S(1)} %get-tuple-element.132), channel_id=1, source_target_pairs={{1,7},{3,5},{5,3},{7,1},{8,14},{10,12},{12,10},{14,8},{16,22},{18,... | collective-permute-start | bytes 393224 | tf_op jit(solution)/shard_map/ppermute | solution.py:663
  197.2 2.1 %collective-permute-done.22.refs_3_ = bf16[2,256,256]{2,1,0:T(8,128)(2,1)S(1)} collective-permute-done((bf16[2,256,256]{2,1,0:T(8,128)(2,1)S(1)}, bf16[2,256,256]{2,1,0:T(8,128)(2,1)S(1)}, u32[]{:S(2)}, u32[]{:S(2)}) %collective-permute-start.22) | collective-permute-done | bytes 262176 | tf_op jit(solution)/shard_map/ppermute | solution.py:419
  200.6 2.2 %collective-permute-done.25.refs_6_ = bf16[256,256]{1,0:T(8,128)(2,1)S(1)} collective-permute-done((bf16[256,256]{1,0:T(8,128)(2,1)S(1)}, bf16[256,256]{1,0:T(8,128)(2,1)S(1)}, u32[]{:S(2)}, u32[]{:S(2)}) %collective-permute-start.25) | collective-permute-done | bytes 131104 | tf_op jit(solution)/shard_map/ppermute | solution.py:663
  202.9 1.7 place.1
  (94 shorter events, 31.4 us)
Async XLA Ops:
  0.6 76.7 %collective-permute-start.10 = (bf16[256,4096]{1,0:T(8,128)(2,1)}, bf16[256,4096]{1,0:T(8,128)(2,1)}, u32[]{:S(2)}, u32[]{:S(2)}) collective-permute-start(bf16[256,4096]{1,0:T(8,128)(2,1)} %refs_28_.1), channel_id=1, source_target_pairs={{0,24},{2,26},{4,28},{6,30},{8,0},{10,2},{12,4},{14,6},{16,8},{18,... | collective-permute-start | bytes 6291464 | tf_op jit(solution)/shard_map/ppermute | solution.py:430
  13.5 22.7 %collective-permute-start = (bf16[272,1024]{1,0:T(8,128)(2,1)}, bf16[272,1024]{1,0:T(8,128)(2,1)S(1)}, u32[]{:S(2)}, u32[]{:S(2)}) collective-permute-start(bf16[272,1024]{1,0:T(8,128)(2,1)} %get-tuple-element.68), channel_id=1, source_target_pairs={{0,2},{2,0},{4,6},{6,4},{8,10},{10,8},{12,14},{14,12},{16,18},{18,... | collective-permute-start | bytes 1671176 | tf_op jit(solution)/shard_map/ppermute | solution.py:419
  14.7 21.6 %collective-permute-start.1 = (bf16[272,1024]{1,0:T(8,128)(2,1)}, bf16[272,1024]{1,0:T(8,128)(2,1)S(1)}, u32[]{:S(2)}, u32[]{:S(2)}) collective-permute-start(bf16[272,1024]{1,0:T(8,128)(2,1)} %get-tuple-element.69), channel_id=1, source_target_pairs={{0,4},{2,6},{4,0},{6,2},{8,12},{10,14},{12,8},{14,10},{16,20},{18,... | collective-permute-start | bytes 1671176 | tf_op jit(solution)/shard_map/ppermute | solution.py:419
  16.0 23.9 %collective-permute-start.2 = (bf16[272,1024]{1,0:T(8,128)(2,1)}, bf16[272,1024]{1,0:T(8,128)(2,1)S(1)}, u32[]{:S(2)}, u32[]{:S(2)}) collective-permute-start(bf16[272,1024]{1,0:T(8,128)(2,1)} %get-tuple-element.70), channel_id=1, source_target_pairs={{0,6},{2,4},{4,2},{6,0},{8,14},{10,12},{12,10},{14,8},{16,22},{18,... | collective-permute-start | bytes 1671176 | tf_op jit(solution)/shard_map/ppermute | solution.py:419
  40.7 49.3 %collective-permute-start.3 = (bf16[256,4480]{1,0:T(8,128)(2,1)S(1)}, bf16[256,4480]{1,0:T(8,128)(2,1)S(1)}, u32[]{:S(2)}, u32[]{:S(2)}) collective-permute-start(bf16[256,4480]{1,0:T(8,128)(2,1)S(1)} %copy-done.1), channel_id=1, source_target_pairs={{0,2},{2,0},{4,6},{6,4},{8,10},{10,8},{12,14},{14,12},{16,18},{18,... | collective-permute-start | bytes 6881288 | tf_op jit(solution)/shard_map/ppermute | solution.py:419
  41.9 49.3 %collective-permute-start.4 = (bf16[256,4480]{1,0:T(8,128)(2,1)S(1)}, bf16[256,4480]{1,0:T(8,128)(2,1)S(1)}, u32[]{:S(2)}, u32[]{:S(2)}) collective-permute-start(bf16[256,4480]{1,0:T(8,128)(2,1)S(1)} %copy-done.1), channel_id=1, source_target_pairs={{0,4},{2,6},{4,0},{6,2},{8,12},{10,14},{12,8},{14,10},{16,20},{18,... | collective-permute-start | bytes 6881288 | tf_op jit(solution)/shard_map/ppermute | solution.py:419
  45.6 10.2 %collective-permute-start.5 = (bf16[144,1024]{1,0:T(8,128)(2,1)}, bf16[144,1024]{1,0:T(8,128)(2,1)S(1)}, u32[]{:S(2)}, u32[]{:S(2)}) collective-permute-start(bf16[144,1024]{1,0:T(8,128)(2,1)} %get-tuple-element.80.refs_0_), channel_id=1, source_target_pairs={{0,8},{2,10},{4,12},{6,14},{8,16},{10,18},{12,20},{14,22},{16,24},... | collective-permute-start | bytes 884744 | tf_op jit(solution)/shard_map/ppermute | solution.py:422
  46.9 8.9 %collective-permute-start.6 = (bf16[144,1024]{1,0:T(8,128)(2,1)}, bf16[144,1024]{1,0:T(8,128)(2,1)S(1)}, u32[]{:S(2)}, u32[]{:S(2)}) collective-permute-start(bf16[144,1024]{1,0:T(8,128)(2,1)} %get-tuple-element.81.refs_2_), channel_id=1, source_target_pairs={{8,0},{10,2},{12,4},{14,6},{16,8},{18,10},{20,12},{22,14},{24,16},... | collective-permute-start | bytes 884744 | tf_op jit(solution)/shard_map/ppermute | solution.py:422
  60.1 17.3 %collective-permute-start.7 = (bf16[144,1024]{1,0:T(8,128)(2,1)}, bf16[144,1024]{1,0:T(8,128)(2,1)S(1)}, u32[]{:S(2)}, u32[]{:S(2)}) collective-permute-start(bf16[144,1024]{1,0:T(8,128)(2,1)} %across.1), channel_id=1, source_target_pairs={{0,16},{2,18},{4,20},{6,22},{8,24},{10,26},{12,28},{14,30},{16,0},... | collective-permute-start | bytes 884744 | tf_op jit(solution)/shard_map/ppermute | solution.py:534
  77.4 48.6 %collective-permute-start.11 = (bf16[256,4096]{1,0:T(8,128)(2,1)}, bf16[256,4096]{1,0:T(8,128)(2,1)}, u32[]{:S(2)}, u32[]{:S(2)}) collective-permute-start(bf16[256,4096]{1,0:T(8,128)(2,1)} %collective-permute-done.10.refs_29_), channel_id=1, source_target_pairs={{0,24},{2,26},{4,28},{6,30},{8,0},{10,2},{12,4},{14,6},{16,8},{18,... | collective-permute-start | bytes 6291464 | tf_op jit(solution)/shard_map/ppermute | solution.py:430
  91.2 24.0 %collective-permute-start.8 = (bf16[128,4480]{1,0:T(8,128)(2,1)S(1)}, bf16[128,4480]{1,0:T(8,128)(2,1)S(1)}, u32[]{:S(2)}, u32[]{:S(2)}) collective-permute-start(bf16[128,4480]{1,0:T(8,128)(2,1)S(1)} %slice.40), channel_id=1, source_target_pairs={{0,4},{2,6},{4,0},{6,2},{8,12},{10,14},{12,8},{14,10},{16,20},{18,... | collective-permute-start | bytes 3440648 | tf_op jit(solution)/shard_map/ppermute | solution.py:419
  92.9 24.1 %collective-permute-start.9 = (bf16[128,4480]{1,0:T(8,128)(2,1)}, bf16[128,4480]{1,0:T(8,128)(2,1)S(1)}, u32[]{:S(2)}, u32[]{:S(2)}) collective-permute-start(bf16[128,4480]{1,0:T(8,128)(2,1)} %slice.41), channel_id=1, source_target_pairs={{0,2},{2,0},{4,6},{6,4},{8,10},{10,8},{12,14},{14,12},{16,18},{18,... | collective-permute-start | bytes 3440648 | tf_op jit(solution)/shard_map/ppermute | solution.py:419
  126.0 50.0 %collective-permute-start.19 = (bf16[256,4096]{1,0:T(8,128)(2,1)}, bf16[256,4096]{1,0:T(8,128)(2,1)S(1)}, u32[]{:S(2)}, u32[]{:S(2)}) collective-permute-start(bf16[256,4096]{1,0:T(8,128)(2,1)} %collective-permute-done.11.refs_9_.refs_30_), channel_id=1, source_target_pairs={{0,24},{2,26},{4,28},{6,30},{8,0},{10,2},{12,4},{14,6},{16,8},{18,... | collective-permute-start | bytes 6291464 | tf_op jit(solution)/shard_map/ppermute | solution.py:430
  130.0 10.6 %collective-permute-start.12 = (bf16[144,1024]{1,0:T(8,128)(2,1)S(1)}, bf16[144,1024]{1,0:T(8,128)(2,1)S(1)}, u32[]{:S(2)}, u32[]{:S(2)}) collective-permute-start(bf16[144,1024]{1,0:T(8,128)(2,1)S(1)} %copy-done.11), channel_id=1, source_target_pairs={{0,2},{2,0},{4,6},{6,4},{8,10},{10,8},{12,14},{14,12},{16,18},{18,... | collective-permute-start | bytes 884744 | tf_op jit(solution)/shard_map/ppermute | solution.py:419
  131.2 9.4 %collective-permute-start.13 = (bf16[144,1024]{1,0:T(8,128)(2,1)S(1)}, bf16[144,1024]{1,0:T(8,128)(2,1)S(1)}, u32[]{:S(2)}, u32[]{:S(2)}) collective-permute-start(bf16[144,1024]{1,0:T(8,128)(2,1)S(1)} %copy-done.11), channel_id=1, source_target_pairs={{0,4},{2,6},{4,0},{6,2},{8,12},{10,14},{12,8},{14,10},{16,20},{18,... | collective-permute-start | bytes 884744 | tf_op jit(solution)/shard_map/ppermute | solution.py:419
  132.5 11.8 %collective-permute-start.14 = (bf16[144,1024]{1,0:T(8,128)(2,1)S(1)}, bf16[144,1024]{1,0:T(8,128)(2,1)S(1)}, u32[]{:S(2)}, u32[]{:S(2)}) collective-permute-start(bf16[144,1024]{1,0:T(8,128)(2,1)S(1)} %copy-done.11), channel_id=1, source_target_pairs={{0,6},{2,4},{4,2},{6,0},{8,14},{10,12},{12,10},{14,8},{16,22},{18,... | collective-permute-start | bytes 884744 | tf_op jit(solution)/shard_map/ppermute | solution.py:419
  145.0 25.4 %copy-start.21 = (bf16[256,128]{1,0:T(8,128)(2,1)S(1)}, bf16[256,128]{1,0:T(8,128)(2,1)}, u32[]{:S(2)}) copy-start(bf16[256,128]{1,0:T(8,128)(2,1)} %get-tuple-element.115) | copy-start | bytes 196612
  145.0 26.3 %copy-start.20 = (bf16[256,128]{1,0:T(8,128)(2,1)S(1)}, bf16[256,128]{1,0:T(8,128)(2,1)}, u32[]{:S(2)}) copy-start(bf16[256,128]{1,0:T(8,128)(2,1)} %get-tuple-element.116) | copy-start | bytes 196612
  145.0 27.0 %copy-start.19 = (bf16[256,128]{1,0:T(8,128)(2,1)S(1)}, bf16[256,128]{1,0:T(8,128)(2,1)}, u32[]{:S(2)}) copy-start(bf16[256,128]{1,0:T(8,128)(2,1)} %get-tuple-element.117) | copy-start | bytes 196612
  145.0 28.1 %copy-start.17 = (f32[256,128]{1,0:T(8,128)S(1)}, f32[256,128]{1,0:T(8,128)}, u32[]{:S(2)}) copy-start(f32[256,128]{1,0:T(8,128)} %get-tuple-element.122) | copy-start | bytes 393220
  167.5 6.5 %collective-permute-start.15 = (bf16[4,2,256,256]{3,2,1,0:T(8,128)(2,1)}, bf16[4,2,256,256]{3,2,1,0:T(8,128)(2,1)S(1)}, u32[]{:S(2)}, u32[]{:S(2)}) collective-permute-start(bf16[4,2,256,256]{3,2,1,0:T(8,128)(2,1)} %get-tuple-element.114), channel_id=1, source_target_pairs={{0,1},{1,0},{2,3},{3,2},{4,5},{5,4},{6,7},{7,6},{8,9},{9,8},{10,11... | collective-permute-start | bytes 3145736 | tf_op jit(solution)/shard_map/ppermute | solution.py:648
  170.4 5.1 %collective-permute-start.16 = (bf16[256,128]{1,0:T(8,128)(2,1)S(1)}, bf16[256,128]{1,0:T(8,128)(2,1)S(1)}, u32[]{:S(2)}, u32[]{:S(2)}) collective-permute-start(bf16[256,128]{1,0:T(8,128)(2,1)S(1)} %copy-done.21), channel_id=1, source_target_pairs={{0,2},{2,0},{4,6},{6,4},{8,10},{10,8},{12,14},{14,12},{16,18},{18,... | collective-permute-start | bytes 196616 | tf_op jit(solution)/shard_map/ppermute | solution.py:419
  171.3 4.2 %collective-permute-start.17 = (bf16[256,128]{1,0:T(8,128)(2,1)S(1)}, bf16[256,128]{1,0:T(8,128)(2,1)S(1)}, u32[]{:S(2)}, u32[]{:S(2)}) collective-permute-start(bf16[256,128]{1,0:T(8,128)(2,1)S(1)} %copy-done.20), channel_id=1, source_target_pairs={{0,4},{2,6},{4,0},{6,2},{8,12},{10,14},{12,8},{14,10},{16,20},{18,... | collective-permute-start | bytes 196616 | tf_op jit(solution)/shard_map/ppermute | solution.py:419
  172.0 4.0 %collective-permute-start.18 = (bf16[256,128]{1,0:T(8,128)(2,1)S(1)}, bf16[256,128]{1,0:T(8,128)(2,1)S(1)}, u32[]{:S(2)}, u32[]{:S(2)}) collective-permute-start(bf16[256,128]{1,0:T(8,128)(2,1)S(1)} %copy-done.19), channel_id=1, source_target_pairs={{0,6},{2,4},{4,2},{6,0},{8,14},{10,12},{12,10},{14,8},{16,22},{18,... | collective-permute-start | bytes 196616 | tf_op jit(solution)/shard_map/ppermute | solution.py:419
  181.8 6.1 %collective-permute-start.23 = (bf16[1024,256]{1,0:T(8,128)(2,1)S(1)}, bf16[1024,256]{1,0:T(8,128)(2,1)S(1)}, u32[]{:S(2)}, u32[]{:S(2)}) collective-permute-start(bf16[1024,256]{1,0:T(8,128)(2,1)S(1)} %convolution_convert_fusion), channel_id=1, source_target_pairs={{0,1},{2,3},{4,5},{6,7},{9,8},{11,10},{13,12},{15,14},{17,16},{19,... | collective-permute-start | bytes 1572872 | tf_op jit(solution)/shard_map/ppermute | solution.py:658
  183.2 4.7 %collective-permute-start.27 = (f32[2,256,128]{2,1,0:T(8,128)S(1)}, f32[2,256,128]{2,1,0:T(8,128)S(1)}, u32[]{:S(2)}, u32[]{:S(2)}) collective-permute-start(f32[2,256,128]{2,1,0:T(8,128)S(1)} %pad_maximum_fusion), channel_id=1, source_target_pairs={{0,1},{1,0},{2,3},{3,2},{4,5},{5,4},{6,7},{7,6},{8,9},{9,8},{10,11... | collective-permute-start | bytes 786440 | tf_op jit(solution)/shard_map/ppermute | solution.py:689
  185.2 8.2 %collective-permute-start.20 = (bf16[2,256,256]{2,1,0:T(8,128)(2,1)S(1)}, bf16[2,256,256]{2,1,0:T(8,128)(2,1)S(1)}, u32[]{:S(2)}, u32[]{:S(2)}) collective-permute-start(bf16[2,256,256]{2,1,0:T(8,128)(2,1)S(1)} %get-tuple-element.130), channel_id=1, source_target_pairs={{0,2},{2,0},{4,6},{6,4},{8,10},{10,8},{12,14},{14,12},{16,18},{18,... | collective-permute-start | bytes 786440 | tf_op jit(solution)/shard_map/ppermute | solution.py:419
  186.4 10.8 %collective-permute-start.21 = (bf16[2,256,256]{2,1,0:T(8,128)(2,1)S(1)}, bf16[2,256,256]{2,1,0:T(8,128)(2,1)S(1)}, u32[]{:S(2)}, u32[]{:S(2)}) collective-permute-start(bf16[2,256,256]{2,1,0:T(8,128)(2,1)S(1)} %get-tuple-element.129), channel_id=1, source_target_pairs={{0,4},{2,6},{4,0},{6,2},{8,12},{10,14},{12,8},{14,10},{16,20},{18,... | collective-permute-start | bytes 786440 | tf_op jit(solution)/shard_map/ppermute | solution.py:419
  186.6 12.7 %collective-permute-start.22 = (bf16[2,256,256]{2,1,0:T(8,128)(2,1)S(1)}, bf16[2,256,256]{2,1,0:T(8,128)(2,1)S(1)}, u32[]{:S(2)}, u32[]{:S(2)}) collective-permute-start(bf16[2,256,256]{2,1,0:T(8,128)(2,1)S(1)} %get-tuple-element.128), channel_id=1, source_target_pairs={{0,6},{2,4},{4,2},{6,0},{8,14},{10,12},{12,10},{14,8},{16,22},{18,... | collective-permute-start | bytes 786440 | tf_op jit(solution)/shard_map/ppermute | solution.py:419
  188.1 12.5 %collective-permute-start.24 = (bf16[256,256]{1,0:T(8,128)(2,1)S(1)}, bf16[256,256]{1,0:T(8,128)(2,1)S(1)}, u32[]{:S(2)}, u32[]{:S(2)}) collective-permute-start(bf16[256,256]{1,0:T(8,128)(2,1)S(1)} %get-tuple-element.134), channel_id=1, source_target_pairs={{1,3},{3,1},{5,7},{7,5},{8,10},{10,8},{12,14},{14,12},{16,18},{18,... | collective-permute-start | bytes 393224 | tf_op jit(solution)/shard_map/ppermute | solution.py:663
  191.2 11.7 %collective-permute-start.25 = (bf16[256,256]{1,0:T(8,128)(2,1)S(1)}, bf16[256,256]{1,0:T(8,128)(2,1)S(1)}, u32[]{:S(2)}, u32[]{:S(2)}) collective-permute-start(bf16[256,256]{1,0:T(8,128)(2,1)S(1)} %get-tuple-element.133), channel_id=1, source_target_pairs={{1,5},{3,7},{5,1},{7,3},{8,12},{10,14},{12,8},{14,10},{16,20},{18,... | collective-permute-start | bytes 393224 | tf_op jit(solution)/shard_map/ppermute | solution.py:663
  193.4 9.5 %collective-permute-start.26 = (bf16[256,256]{1,0:T(8,128)(2,1)S(1)}, bf16[256,256]{1,0:T(8,128)(2,1)S(1)}, u32[]{:S(2)}, u32[]{:S(2)}) collective-permute-start(bf16[256,256]{1,0:T(8,128)(2,1)S(1)} %get-tuple-element.132), channel_id=1, source_target_pairs={{1,7},{3,5},{5,3},{7,1},{8,14},{10,12},{12,10},{14,8},{16,22},{18,... | collective-permute-start | bytes 393224 | tf_op jit(solution)/shard_map/ppermute | solution.py:663
  (18 other events, 89.4 us)
where the time goes:
time: 206 us; the launch traced here: 205 us
  Pallas kernels  91.5 us (44%)
  waiting for transfers between devices  50.4 us (24%)
  starting transfers between devices  46.1 us (22%)
  local copies, waits for them, and re-layouts  6.54 us (3%)
  matrix products  5.79 us (3%)
  other arithmetic  3.2 us (2%)
    pallas_call x12, Pallas kernels, call(): return lambda *operands: fn(*operands, *after)  89.8 us
    ppermute x16, waiting for transfers between devices, swap(): return lax.ppermute(value, 'seq', [(s, s ^ j) for s in range(n_seq)])  24.2 us
    ppermute x1, waiting for transfers between devices, local(): got = lax.ppermute(across, 'seq', [(s, s ^ d * RING) for s in range(n_seq)])  13.4 us
    ppermute x16, starting transfers between devices, swap(): return lax.ppermute(value, 'seq', [(s, s ^ j) for s in range(n_seq)])  13.1 us
    ppermute x3, starting transfers between devices, turn_w(): w_blocks.append(lax.ppermute(w_blocks[-1], 'seq', turn))  12 us
    ppermute x3, starting transfers between devices, local(): lax.ppermute(tile[j], both_axes, [(2 * s + owner(s), 2 * (s ^ j) + owner(...  8.37 us
    ppermute x2, waiting for transfers between devices, along(): lax.ppermute(value, 'seq', [(s, s + d * RING) for s in range(n_seq) if 0...  7.65 us
    dot_general x1, matrix products, mm(): return lax.dot_general(a, b, dims, preferred_element_type=f32)  5.79 us
  transfers between devices with their start and end apart: 28, of which 13 were waited for; matrix products, arithmetic and copies ran while one was open for 3% of the time, Pallas kernels for 44%

commit v1 on v0

--- a/solution.py
+++ b/solution.py
@@ -358,6 +358,16 @@
             outs[j][at_rows] = mm(scaled, states, NT).astype(bf16)
 
 
+def early_kernel(at, mine, got, *refs):
+    reads, outs = refs[:RING], refs[RING:]
+    width = mine.shape[3]
+    for j in range(RING):
+        for slot in range(mine.shape[1]):
+            value = mine[j, slot].astype(f32) + got[j, slot].astype(f32)
+            outs[j][:, slot * width : (slot + 1) * width] = value.astype(bf16)
+        outs[j][:, mine.shape[1] * width :] = reads[j][...]
+
+
 def place_kernel(outer, share, at, *refs):
     blocks, late, out = refs[:RING], refs[RING:-1], refs[-1]
     p, z, side = at[0], at[1], at[2]
@@ -373,7 +383,7 @@
 
             @pl.when(side * share + slot != last)
             def _():
-                out[:, pl.ds(column, width)] = blocks[j][slot]
+                out[:, pl.ds(column, width)] = blocks[j][:, slot * width : (slot + 1) * width]
 
 
 def call(kernel, name, grid, in_specs, out_specs, out_shape, scratch=(), after=()):
@@ -646,9 +656,16 @@
     if two:
         mine, theirs = tiles
         got = lax.ppermute(theirs, "head", [(0, 1), (1, 0)])
-        early = (mine.astype(f32) + got.astype(f32)).astype(bf16)
-        read_got = [swap(read_parts[j], j) for j in range(1, RING)]
-        early, read_got, w_last = lax.optimization_barrier((early, read_got, w_blocks[-1]))
+        pack_width = share * w_rows + state_dim
+        early = call(
+            early_kernel,
+            "early_sums",
+            (1,),
+            [const(*mine.shape)] * 2 + [proj_spec] * RING,
+            [const(rows, pack_width)] * RING,
+            [shape((rows, pack_width), bf16)] * RING,
+        )(at, mine, got, *read_parts)
+        early, w_last = lax.optimization_barrier((early, w_blocks[-1]))
         tile = mm(acts, w_last, NT).astype(bf16)
 
         def owner(s):
@@ -668,6 +685,7 @@
             for j in range(1, RING)
         ]
         early = to_owners(early)
+        read_got = [v[:, share * w_rows :] for v in early[1:]]
         input_grad = pl.pallas_call(
             functools.partial(place_kernel, outer, share),
             in_specs=[pl.BlockSpec(memory_space=pltpu.SMEM)]

time: 206 us -> 211 us (1.024)
  waiting for transfers between devices: 50.4 us -> 57 us
  starting transfers between devices: 46.1 us -> 42.8 us
  Pallas kernels: 91.5 us -> 94.8 us
  other arithmetic: 3.2 us -> 0.83 us
    ppermute x16 -> x13, waiting for transfers between devices: 24.2 us -> 28.8 us  [swap(): return lax.ppermute(value, 'seq', [(s, s ^ j) for s in range(n_seq)])]
    pallas_call x12 -> x13, Pallas kernels: 89.8 us -> 93.1 us  [call(): return lambda *operands: fn(*operands, *after)]
    ppermute x16 -> x13, starting transfers between devices: 13.1 us -> 10.4 us  [swap(): return lax.ppermute(value, 'seq', [(s, s ^ j) for s in range(n_seq)])]
    ppermute x1, waiting for transfers between devices: 0.01 us -> 2.5 us  [local(): got = lax.ppermute(theirs, 'head', [(0, 1), (1, 0)])]
  transfers between devices with their start and end apart: 28 -> 25, of which waited for: 13 -> 12; matrix products, arithmetic and copies ran while one was open for 3% -> 4% of each run, Pallas kernels for 44% -> 44%
where the time goes in v1:
time: 211 us; the launch traced here: 210 us
  Pallas kernels  94.8 us (45%)
  waiting for transfers between devices  57 us (27%)
  starting transfers between devices  42.8 us (20%)
  local copies, waits for them, and re-layouts  7.48 us (4%)
  matrix products  5.8 us (3%)
    pallas_call x13, Pallas kernels, call(): return lambda *operands: fn(*operands, *after)  93.1 us
    ppermute x13, waiting for transfers between devices, swap(): return lax.ppermute(value, 'seq', [(s, s ^ j) for s in range(n_seq)])  28.8 us
    ppermute x1, waiting for transfers between devices, local(): got = lax.ppermute(across, 'seq', [(s, s ^ d * RING) for s in range(n_seq)])  13.3 us
    ppermute x3, starting transfers between devices, turn_w(): w_blocks.append(lax.ppermute(w_blocks[-1], 'seq', turn))  12.1 us
    ppermute x13, starting transfers between devices, swap(): return lax.ppermute(value, 'seq', [(s, s ^ j) for s in range(n_seq)])  10.4 us
    ppermute x3, starting transfers between devices, local(): lax.ppermute(tile[j], both_axes, [(2 * s + owner(s), 2 * (s ^ j) + owner(...  8.37 us
    ppermute x2, waiting for transfers between devices, along(): lax.ppermute(value, 'seq', [(s, s + d * RING) for s in range(n_seq) if 0...  7.63 us
    dot_general x1, matrix products, mm(): return lax.dot_general(a, b, dims, preferred_element_type=f32)  5.8 us
  transfers between devices with their start and end apart: 25, of which 12 were waited for; matrix products, arithmetic and copies ran while one was open for 4% of the time, Pallas kernels for 44%

profile of v1, /device:TPU:1, one launch (start us, length us, event | category | flops | bytes accessed | tf_op | source)
XLA Modules:
  0.0 209.6 jit_solution(14450584765388330948)
XLA Ops:
  0.6 4.2 %collective-permute-start.10 = (bf16[256,4096]{1,0:T(8,128)(2,1)}, bf16[256,4096]{1,0:T(8,128)(2,1)}, u32[]{:S(2)}, u32[]{:S(2)}) collective-permute-start(bf16[256,4096]{1,0:T(8,128)(2,1)} %refs_28_.1), channel_id=1, source_target_pairs={{0,24},{2,26},{4,28},{6,30},{8,0},{10,2},{12,4},{14,6},{16,8},{18,... | collective-permute-start | bytes 6291464 | tf_op jit(solution)/shard_map/ppermute | solution.py:440
  5.4 8.1 %edges.1 = (bf16[272,1024]{1,0:T(8,128)(2,1)}, bf16[272,1024]{1,0:T(8,128)(2,1)}, bf16[272,1024]{1,0:T(8,128)(2,1)}, bf16[272,1024]{1,0:T(8,128)(2,1)}) custom-call(s32[3]{0:T(128)} %pad_add_fusion.at, bf16[256,4096]{1,0:T(8,128)(2,1)} %refs_31_.1, bf16[256,4096]{1,0:T(8,128)(2,1)} %refs_1_.5, bf16[256,128]{1,0:T(8,128)(2,1)} %refs_2_.5, ...), custom_call_target="tpu_custom_call" | custom-call | tf_op jit(solution)/shard_map/edges/pallas_call | solution.py:409
  16.2 3.8 %pack.1.refs_0_.refs_1_.refs_2_.refs_3_.refs_4_.refs_5_.refs_6_.refs_7_.refs_16_.refs_20_ = bf16[256,4480]{1,0:T(8,128)(2,1)} custom-call(s32[3]{0:T(128)} %pad_add_fusion.at, bf16[256,4096]{1,0:T(8,128)(2,1)} %refs_1_.5, bf16[256,128]{1,0:T(8,128)(2,1)} %refs_2_.5, bf16[256,128]{1,0:T(8,128)(2,1)} %refs_3_.3, f32[32,256]{1,0:T(8,128)} %bitcast.15), custom_call_target="tpu_custom_call" | custom-call | tf_op jit(solution)/shard_map/pack/pallas_call | solution.py:409
  20.0 8.2 %own_tokens.1 = (f32[256,128]{1,0:T(8,128)}, f32[256,128]{1,0:T(8,128)}) custom-call(s32[3]{0:T(128)} %pad_add_fusion.at, bf16[256,4096]{1,0:T(8,128)(2,1)} %refs_31_.1, bf16[256,4096]{1,0:T(8,128)(2,1)} %refs_1_.5, bf16[256,128]{1,0:T(8,128)(2,1)} %refs_2_.5, bf16[256,128]{1,0:T(8,128)(2,1)} %refs_3_.3, f32[32,256]{1,0:T(8,128)} %bitcast.16), custom_call_target="tpu_custom_call" | custom-call | tf_op jit(solution)/shard_map/own_tokens/pallas_call | solution.py:409
  28.2 8.1 %tokens.4 = (bf16[256,4096]{1,0:T(8,128)(2,1)}, bf16[4,128,1024]{2,1,0:T(8,128)(2,1)}, f32[1,4096]{1,0:T(1,128)}, f32[256,128]{1,0:T(8,128)}) custom-call(s32[3]{0:T(128)} %pad_add_fusion.at, bf16[256,4480]{1,0:T(8,128)(2,1)} %pack.1.refs_0_.refs_1_.refs_2_.refs_3_.refs_4_.refs_5_.refs_6_.refs_7_.refs_16_.refs_20_, ...), custom_call_target="tpu_custom_call" | custom-call | tf_op jit(solution)/shard_map/tokens/pallas_call | solution.py:409
  36.4 3.5 %collective-permute-done.2.refs_3_.refs_16_ = bf16[272,1024]{1,0:T(8,128)(2,1)S(1)} collective-permute-done((bf16[272,1024]{1,0:T(8,128)(2,1)}, bf16[272,1024]{1,0:T(8,128)(2,1)S(1)}, u32[]{:S(2)}, u32[]{:S(2)}) %collective-permute-start.2) | collective-permute-done | bytes 557088 | tf_op jit(solution)/shard_map/ppermute | solution.py:429
  42.1 3.4 %messages.1 = (bf16[144,1024]{1,0:T(8,128)(2,1)}, bf16[144,1024]{1,0:T(8,128)(2,1)}) custom-call(s32[3]{0:T(128)} %pad_add_fusion.at, bf16[272,1024]{1,0:T(8,128)(2,1)} %get-tuple-element.80.refs_0_.refs_13_, bf16[272,1024]{1,0:T(8,128)(2,1)} %copy-done.7, bf16[272,1024]{1,0:T(8,128)(2,1)} %copy-done.8, bf16[272,1024]{1,0:T(8,128)(2,1)} %copy-done.9), custom_call_target="tpu_custom_call" | custom-call | tf_op jit(solution)/shard_map/messages/pallas_call | solution.py:409
  48.2 7.6 %collective-permute-done.5.refs_1_.refs_0_ = bf16[144,1024]{1,0:T(8,128)(2,1)S(1)} collective-permute-done((bf16[144,1024]{1,0:T(8,128)(2,1)}, bf16[144,1024]{1,0:T(8,128)(2,1)S(1)}, u32[]{:S(2)}, u32[]{:S(2)}) %collective-permute-start.5) | collective-permute-done | bytes 294944 | tf_op jit(solution)/shard_map/ppermute | solution.py:432
  57.2 2.8 %across.1 = bf16[144,1024]{1,0:T(8,128)(2,1)} custom-call(s32[3]{0:T(128)} %pad_add_fusion.at, bf16[144,1024]{1,0:T(8,128)(2,1)} %get-tuple-element.84.refs_0_, bf16[144,1024]{1,0:T(8,128)(2,1)} %copy-done.10, bf16[144,1024]{1,0:T(8,128)(2,1)} %get-tuple-element.85.refs_2_, bf16[144,1024]{1,0:T(8,128)(2,1)} %copy-done.11), custom_call_target="tpu_custom_call" | custom-call | tf_op jit(solution)/shard_map/across/pallas_call | solution.py:409
  60.1 3.9 %collective-permute-start.7 = (bf16[144,1024]{1,0:T(8,128)(2,1)}, bf16[144,1024]{1,0:T(8,128)(2,1)S(1)}, u32[]{:S(2)}, u32[]{:S(2)}) collective-permute-start(bf16[144,1024]{1,0:T(8,128)(2,1)} %across.1), channel_id=1, source_target_pairs={{0,16},{2,18},{4,20},{6,22},{8,24},{10,26},{12,28},{14,30},{16,0},... | collective-permute-start | bytes 884744 | tf_op jit(solution)/shard_map/ppermute | solution.py:544
  64.0 13.3 %collective-permute-done.7.refs_2_ = bf16[144,1024]{1,0:T(8,128)(2,1)S(1)} collective-permute-done((bf16[144,1024]{1,0:T(8,128)(2,1)}, bf16[144,1024]{1,0:T(8,128)(2,1)S(1)}, u32[]{:S(2)}, u32[]{:S(2)}) %collective-permute-start.7) | collective-permute-done | bytes 294944 | tf_op jit(solution)/shard_map/ppermute | solution.py:544
  77.4 3.9 %collective-permute-start.11 = (bf16[256,4096]{1,0:T(8,128)(2,1)}, bf16[256,4096]{1,0:T(8,128)(2,1)}, u32[]{:S(2)}, u32[]{:S(2)}) collective-permute-start(bf16[256,4096]{1,0:T(8,128)(2,1)} %collective-permute-done.10.refs_29_), channel_id=1, source_target_pairs={{0,24},{2,26},{4,28},{6,30},{8,0},{10,2},{12,4},{14,6},{16,8},{18,... | collective-permute-start | bytes 6291464 | tf_op jit(solution)/shard_map/ppermute | solution.py:440
  81.2 2.7 %settle.1 = (bf16[144,1024]{1,0:T(8,128)(2,1)}, bf16[144,1024]{1,0:T(8,128)(2,1)}) custom-call(s32[3]{0:T(128)} %pad_add_fusion.at, bf16[144,1024]{1,0:T(8,128)(2,1)} %copy-done.10, bf16[144,1024]{1,0:T(8,128)(2,1)} %copy-done.11, bf16[144,1024]{1,0:T(8,128)(2,1)} %copy-done.18), custom_call_target="tpu_custom_call" | custom-call | tf_op jit(solution)/shard_map/settle/pallas_call | solution.py:409
  84.0 6.1 %collective-permute-done.3.refs_0_.refs_1_.refs_2_.refs_3_.refs_4_.refs_5_.refs_6_.refs_7_.refs_17_.refs_21_ = bf16[256,4480]{1,0:T(8,128)(2,1)S(1)} collective-permute-done((bf16[256,4480]{1,0:T(8,128)(2,1)S(1)}, bf16[256,4480]{1,0:T(8,128)(2,1)S(1)}, u32[]{:S(2)}, u32[]{:S(2)}) %collective-permute-start.3) | collective-permute-done | bytes 2293792 | tf_op jit(solution)/shard_map/ppermute | solution.py:429
  93.9 8.0 %tokens.6 = (bf16[256,4096]{1,0:T(8,128)(2,1)}, bf16[4,128,1024]{2,1,0:T(8,128)(2,1)}, f32[1,4096]{1,0:T(1,128)}, f32[256,128]{1,0:T(8,128)}) custom-call(s32[3]{0:T(128)} %pad_add_fusion.at, bf16[256,4480]{1,0:T(8,128)(2,1)} %copy-done.4, bf16[256,4480]{1,0:T(8,128)(2,1)} %copy-done.4, bf16[256,4480]{1,0:T(8,128)(2,1)} %copy-done.4, ...), custom_call_target="tpu_custom_call" | custom-call | tf_op jit(solution)/shard_map/tokens/pallas_call | solution.py:409
  101.9 8.0 %tokens.5 = (bf16[256,4096]{1,0:T(8,128)(2,1)}, bf16[4,128,1024]{2,1,0:T(8,128)(2,1)}, f32[1,4096]{1,0:T(1,128)}, f32[256,128]{1,0:T(8,128)}) custom-call(s32[3]{0:T(128)} %pad_add_fusion.at, bf16[256,4480]{1,0:T(8,128)(2,1)} %copy-done.3, bf16[256,4480]{1,0:T(8,128)(2,1)} %copy-done.3, bf16[256,4480]{1,0:T(8,128)(2,1)} %copy-done.3, ...), custom_call_target="tpu_custom_call" | custom-call | tf_op jit(solution)/shard_map/tokens/pallas_call | solution.py:409
  109.9 5.3 %collective-permute-done.8.refs_3_.refs_11_.refs_0_.refs_2_.refs_4_.refs_6_.refs_19_ = bf16[128,4480]{1,0:T(8,128)(2,1)S(1)} collective-permute-done((bf16[128,4480]{1,0:T(8,128)(2,1)S(1)}, bf16[128,4480]{1,0:T(8,128)(2,1)S(1)}, u32[]{:S(2)}, u32[]{:S(2)}) %collective-permute-start.8) | collective-permute-done | bytes 1146912 | tf_op jit(solution)/shard_map/ppermute | solution.py:429
  115.2 1.9 collective-permute-done.9.refs_7_.refs_12_.refs_1_.refs_3_.refs_5_.refs_23_
  118.1 6.3 %read_carry.1 = (bf16[256,128]{1,0:T(8,128)(2,1)}, bf16[256,128]{1,0:T(8,128)(2,1)}, bf16[256,128]{1,0:T(8,128)(2,1)}, bf16[256,128]{1,0:T(8,128)(2,1)}) custom-call(s32[3]{0:T(128)} %pad_add_fusion.at, bf16[256,4480]{1,0:T(8,128)(2,1)} %pack.1.refs_0_.refs_1_.refs_2_.refs_3_.refs_4_.refs_5_.refs_6_.refs_7_.refs_16_.refs_20_, bf16[256,4480]{1,0:T(8,128)(2,1)} %copy-done.3, ...), custom_call_target="tpu_custom_call" | custom-call | tf_op jit(solution)/shard_map/read_carry/pallas_call | solution.py:409
  126.0 4.0 %collective-permute-start.16 = (bf16[256,4096]{1,0:T(8,128)(2,1)}, bf16[256,4096]{1,0:T(8,128)(2,1)S(1)}, u32[]{:S(2)}, u32[]{:S(2)}) collective-permute-start(bf16[256,4096]{1,0:T(8,128)(2,1)} %collective-permute-done.11.refs_9_.refs_30_), channel_id=1, source_target_pairs={{0,24},{2,26},{4,28},{6,30},{8,0},{10,2},{12,4},{14,6},{16,8},{18,... | collective-permute-start | bytes 6291464 | tf_op jit(solution)/shard_map/ppermute | solution.py:440
  132.7 8.0 %tokens.7 = (bf16[256,4096]{1,0:T(8,128)(2,1)}, bf16[4,128,1024]{2,1,0:T(8,128)(2,1)}, f32[1,4096]{1,0:T(1,128)}, f32[256,128]{1,0:T(8,128)}) custom-call(s32[3]{0:T(128)} %pad_add_fusion.at, bf16[128,4480]{1,0:T(8,128)(2,1)} %copy-done.5, bf16[128,4480]{1,0:T(8,128)(2,1)} %copy-done.6, bf16[128,4480]{1,0:T(8,128)(2,1)} %copy-done.5, ...), custom_call_target="tpu_custom_call" | custom-call | tf_op jit(solution)/shard_map/tokens/pallas_call | solution.py:409
  140.7 3.6 %collective-permute-done.14.refs_11_ = bf16[144,1024]{1,0:T(8,128)(2,1)S(1)} collective-permute-done((bf16[144,1024]{1,0:T(8,128)(2,1)S(1)}, bf16[144,1024]{1,0:T(8,128)(2,1)S(1)}, u32[]{:S(2)}, u32[]{:S(2)}) %collective-permute-start.14) | collective-permute-done | bytes 294944 | tf_op jit(solution)/shard_map/ppermute | solution.py:429
  145.0 22.3 %finish.1 = (bf16[1024,4096]{1,0:T(8,128)(2,1)}, bf16[256,4096]{1,0:T(8,128)(2,1)}, f32[256,128]{1,0:T(8,128)}, bf16[4,2,256,256]{3,2,1,0:T(8,128)(2,1)}, bf16[4,2,256,256]{3,2,1,0:T(8,128)(2,1)}) custom-call(s32[3]{0:T(128)} %pad_add_fusion.at, bf16[256,4096]{1,0:T(8,128)(2,1)} %get-tuple-element.70.refs_0_, bf16[256,4096]{1,0:T(8,128)(2,1)} %get-tuple-element.88.refs_1_, ...), custom_call_target="tpu_custom_call" | custom-call | tf_op jit(solution)/shard_map/finish/pallas_call | solution.py:409
  167.3 2.9 %collective-permute-start.15 = (bf16[4,2,256,256]{3,2,1,0:T(8,128)(2,1)}, bf16[4,2,256,256]{3,2,1,0:T(8,128)(2,1)S(1)}, u32[]{:S(2)}, u32[]{:S(2)}) collective-permute-start(bf16[4,2,256,256]{3,2,1,0:T(8,128)(2,1)} %get-tuple-element.118), channel_id=1, source_target_pairs={{0,1},{1,0},{2,3},{3,2},{4,5},{5,4},{6,7},{7,6},{8,9},{9,8},{10,11... | collective-permute-start | bytes 3145736 | tf_op jit(solution)/shard_map/ppermute | solution.py:658
  170.2 2.5 %collective-permute-done.15.refs_1_ = bf16[4,2,256,256]{3,2,1,0:T(8,128)(2,1)S(1)} collective-permute-done((bf16[4,2,256,256]{3,2,1,0:T(8,128)(2,1)}, bf16[4,2,256,256]{3,2,1,0:T(8,128)(2,1)S(1)}, u32[]{:S(2)}, u32[]{:S(2)}) %collective-permute-start.15) | collective-permute-done | bytes 1048608 | tf_op jit(solution)/shard_map/ppermute | solution.py:658
  173.7 3.3 %early_sums.1 = (bf16[256,640]{1,0:T(8,128)(2,1)}, bf16[256,640]{1,0:T(8,128)(2,1)}, bf16[256,640]{1,0:T(8,128)(2,1)}, bf16[256,640]{1,0:T(8,128)(2,1)}) custom-call(s32[3]{0:T(128)} %pad_add_fusion.at, bf16[4,2,256,256]{3,2,1,0:T(8,128)(2,1)} %get-tuple-element.117.refs_0_, bf16[4,2,256,256]{3,2,1,0:T(8,128)(2,1)} %copy-done.12, ...), custom_call_target="tpu_custom_call" | custom-call | tf_op jit(solution)/shard_map/early_sums/pallas_call | solution.py:409
  179.7 5.8 %convolution_convert_fusion = bf16[1024,256]{1,0:T(8,128)(2,1)S(1)} fusion(bf16[1024,4096]{1,0:T(8,128)(2,1)} %get-tuple-element.130, bf16[256,4096]{1,0:T(8,128)(2,1)S(1)} %collective-permute-done.16), kind=kOutput, calls=%fused_computation | convolution fusion | flops 2147745792 | bytes 11010048 | tf_op jit(solution)/shard_map/dot_general | solution.py:20
  186.8 7.4 %collective-permute-done.19.refs_3_ = bf16[256,640]{1,0:T(8,128)(2,1)S(1)} collective-permute-done((bf16[256,640]{1,0:T(8,128)(2,1)}, bf16[256,640]{1,0:T(8,128)(2,1)S(1)}, u32[]{:S(2)}, u32[]{:S(2)}) %collective-permute-start.19) | collective-permute-done | bytes 327712 | tf_op jit(solution)/shard_map/ppermute | solution.py:429
  195.8 2.3 %collective-permute-start.21 = (bf16[256,256]{1,0:T(8,128)(2,1)S(1)}, bf16[256,256]{1,0:T(8,128)(2,1)S(1)}, u32[]{:S(2)}, u32[]{:S(2)}) collective-permute-start(bf16[256,256]{1,0:T(8,128)(2,1)S(1)} %get-tuple-element.138), channel_id=1, source_target_pairs={{1,3},{3,1},{5,7},{7,5},{8,10},{10,8},{12,14},{14,12},{16,18},{18,... | collective-permute-start | bytes 393224 | tf_op jit(solution)/shard_map/ppermute | solution.py:680
  198.1 3.2 %collective-permute-start.22 = (bf16[256,256]{1,0:T(8,128)(2,1)S(1)}, bf16[256,256]{1,0:T(8,128)(2,1)S(1)}, u32[]{:S(2)}, u32[]{:S(2)}) collective-permute-start(bf16[256,256]{1,0:T(8,128)(2,1)S(1)} %get-tuple-element.137), channel_id=1, source_target_pairs={{1,5},{3,7},{5,1},{7,3},{8,12},{10,14},{12,8},{14,10},{16,20},{18,... | collective-permute-start | bytes 393224 | tf_op jit(solution)/shard_map/ppermute | solution.py:680
  201.4 2.8 %collective-permute-start.23 = (bf16[256,256]{1,0:T(8,128)(2,1)S(1)}, bf16[256,256]{1,0:T(8,128)(2,1)S(1)}, u32[]{:S(2)}, u32[]{:S(2)}) collective-permute-start(bf16[256,256]{1,0:T(8,128)(2,1)S(1)} %get-tuple-element.136), channel_id=1, source_target_pairs={{1,7},{3,5},{5,3},{7,1},{8,14},{10,12},{12,10},{14,8},{16,22},{18,... | collective-permute-start | bytes 393224 | tf_op jit(solution)/shard_map/ppermute | solution.py:680
  204.9 3.0 %collective-permute-done.23.refs_7_ = bf16[256,256]{1,0:T(8,128)(2,1)S(1)} collective-permute-done((bf16[256,256]{1,0:T(8,128)(2,1)S(1)}, bf16[256,256]{1,0:T(8,128)(2,1)S(1)}, u32[]{:S(2)}, u32[]{:S(2)}) %collective-permute-start.23) | collective-permute-done | bytes 131104 | tf_op jit(solution)/shard_map/ppermute | solution.py:680
  (87 shorter events, 28.3 us)
Async XLA Ops:
  0.6 76.7 %collective-permute-start.10 = (bf16[256,4096]{1,0:T(8,128)(2,1)}, bf16[256,4096]{1,0:T(8,128)(2,1)}, u32[]{:S(2)}, u32[]{:S(2)}) collective-permute-start(bf16[256,4096]{1,0:T(8,128)(2,1)} %refs_28_.1), channel_id=1, source_target_pairs={{0,24},{2,26},{4,28},{6,30},{8,0},{10,2},{12,4},{14,6},{16,8},{18,... | collective-permute-start | bytes 6291464 | tf_op jit(solution)/shard_map/ppermute | solution.py:440
  13.5 22.8 %collective-permute-start = (bf16[272,1024]{1,0:T(8,128)(2,1)}, bf16[272,1024]{1,0:T(8,128)(2,1)S(1)}, u32[]{:S(2)}, u32[]{:S(2)}) collective-permute-start(bf16[272,1024]{1,0:T(8,128)(2,1)} %get-tuple-element.72), channel_id=1, source_target_pairs={{0,2},{2,0},{4,6},{6,4},{8,10},{10,8},{12,14},{14,12},{16,18},{18,... | collective-permute-start | bytes 1671176 | tf_op jit(solution)/shard_map/ppermute | solution.py:429
  14.8 21.6 %collective-permute-start.1 = (bf16[272,1024]{1,0:T(8,128)(2,1)}, bf16[272,1024]{1,0:T(8,128)(2,1)S(1)}, u32[]{:S(2)}, u32[]{:S(2)}) collective-permute-start(bf16[272,1024]{1,0:T(8,128)(2,1)} %get-tuple-element.73), channel_id=1, source_target_pairs={{0,4},{2,6},{4,0},{6,2},{8,12},{10,14},{12,8},{14,10},{16,20},{18,... | collective-permute-start | bytes 1671176 | tf_op jit(solution)/shard_map/ppermute | solution.py:429
  16.0 23.9 %collective-permute-start.2 = (bf16[272,1024]{1,0:T(8,128)(2,1)}, bf16[272,1024]{1,0:T(8,128)(2,1)S(1)}, u32[]{:S(2)}, u32[]{:S(2)}) collective-permute-start(bf16[272,1024]{1,0:T(8,128)(2,1)} %get-tuple-element.74), channel_id=1, source_target_pairs={{0,6},{2,4},{4,2},{6,0},{8,14},{10,12},{12,10},{14,8},{16,22},{18,... | collective-permute-start | bytes 1671176 | tf_op jit(solution)/shard_map/ppermute | solution.py:429
  28.2 12.5 %copy-start.2 = (bf16[256,4480]{1,0:T(8,128)(2,1)S(1)}, bf16[256,4480]{1,0:T(8,128)(2,1)}, u32[]{:S(2)}) copy-start(bf16[256,4480]{1,0:T(8,128)(2,1)} %pack.1.refs_0_.refs_1_.refs_2_.refs_3_.refs_4_.refs_5_.refs_6_.refs_7_.refs_16_.refs_20_) | copy-start | bytes 6881284
  40.7 49.3 %collective-permute-start.3 = (bf16[256,4480]{1,0:T(8,128)(2,1)S(1)}, bf16[256,4480]{1,0:T(8,128)(2,1)S(1)}, u32[]{:S(2)}, u32[]{:S(2)}) collective-permute-start(bf16[256,4480]{1,0:T(8,128)(2,1)S(1)} %copy-done.2), channel_id=1, source_target_pairs={{0,2},{2,0},{4,6},{6,4},{8,10},{10,8},{12,14},{14,12},{16,18},{18,... | collective-permute-start | bytes 6881288 | tf_op jit(solution)/shard_map/ppermute | solution.py:429
  41.9 49.3 %collective-permute-start.4 = (bf16[256,4480]{1,0:T(8,128)(2,1)S(1)}, bf16[256,4480]{1,0:T(8,128)(2,1)S(1)}, u32[]{:S(2)}, u32[]{:S(2)}) collective-permute-start(bf16[256,4480]{1,0:T(8,128)(2,1)S(1)} %copy-done.2), channel_id=1, source_target_pairs={{0,4},{2,6},{4,0},{6,2},{8,12},{10,14},{12,8},{14,10},{16,20},{18,... | collective-permute-start | bytes 6881288 | tf_op jit(solution)/shard_map/ppermute | solution.py:429
  45.6 10.2 %collective-permute-start.5 = (bf16[144,1024]{1,0:T(8,128)(2,1)}, bf16[144,1024]{1,0:T(8,128)(2,1)S(1)}, u32[]{:S(2)}, u32[]{:S(2)}) collective-permute-start(bf16[144,1024]{1,0:T(8,128)(2,1)} %get-tuple-element.84.refs_0_), channel_id=1, source_target_pairs={{0,8},{2,10},{4,12},{6,14},{8,16},{10,18},{12,20},{14,22},{16,24},... | collective-permute-start | bytes 884744 | tf_op jit(solution)/shard_map/ppermute | solution.py:432
  46.9 8.9 %collective-permute-start.6 = (bf16[144,1024]{1,0:T(8,128)(2,1)}, bf16[144,1024]{1,0:T(8,128)(2,1)S(1)}, u32[]{:S(2)}, u32[]{:S(2)}) collective-permute-start(bf16[144,1024]{1,0:T(8,128)(2,1)} %get-tuple-element.85.refs_2_), channel_id=1, source_target_pairs={{8,0},{10,2},{12,4},{14,6},{16,8},{18,10},{20,12},{22,14},{24,16},... | collective-permute-start | bytes 884744 | tf_op jit(solution)/shard_map/ppermute | solution.py:432
  60.1 17.3 %collective-permute-start.7 = (bf16[144,1024]{1,0:T(8,128)(2,1)}, bf16[144,1024]{1,0:T(8,128)(2,1)S(1)}, u32[]{:S(2)}, u32[]{:S(2)}) collective-permute-start(bf16[144,1024]{1,0:T(8,128)(2,1)} %across.1), channel_id=1, source_target_pairs={{0,16},{2,18},{4,20},{6,22},{8,24},{10,26},{12,28},{14,30},{16,0},... | collective-permute-start | bytes 884744 | tf_op jit(solution)/shard_map/ppermute | solution.py:544
  77.4 48.6 %collective-permute-start.11 = (bf16[256,4096]{1,0:T(8,128)(2,1)}, bf16[256,4096]{1,0:T(8,128)(2,1)}, u32[]{:S(2)}, u32[]{:S(2)}) collective-permute-start(bf16[256,4096]{1,0:T(8,128)(2,1)} %collective-permute-done.10.refs_29_), channel_id=1, source_target_pairs={{0,24},{2,26},{4,28},{6,30},{8,0},{10,2},{12,4},{14,6},{16,8},{18,... | collective-permute-start | bytes 6291464 | tf_op jit(solution)/shard_map/ppermute | solution.py:440
  91.2 24.0 %collective-permute-start.8 = (bf16[128,4480]{1,0:T(8,128)(2,1)S(1)}, bf16[128,4480]{1,0:T(8,128)(2,1)S(1)}, u32[]{:S(2)}, u32[]{:S(2)}) collective-permute-start(bf16[128,4480]{1,0:T(8,128)(2,1)S(1)} %slice.37), channel_id=1, source_target_pairs={{0,4},{2,6},{4,0},{6,2},{8,12},{10,14},{12,8},{14,10},{16,20},{18,... | collective-permute-start | bytes 3440648 | tf_op jit(solution)/shard_map/ppermute | solution.py:429
  93.0 24.1 %collective-permute-start.9 = (bf16[128,4480]{1,0:T(8,128)(2,1)}, bf16[128,4480]{1,0:T(8,128)(2,1)S(1)}, u32[]{:S(2)}, u32[]{:S(2)}) collective-permute-start(bf16[128,4480]{1,0:T(8,128)(2,1)} %slice.38), channel_id=1, source_target_pairs={{0,2},{2,0},{4,6},{6,4},{8,10},{10,8},{12,14},{14,12},{16,18},{18,... | collective-permute-start | bytes 3440648 | tf_op jit(solution)/shard_map/ppermute | solution.py:429
  118.1 11.9 %copy-start.14 = (bf16[144,1024]{1,0:T(8,128)(2,1)S(1)}, bf16[144,1024]{1,0:T(8,128)(2,1)}, u32[]{:S(2)}) copy-start(bf16[144,1024]{1,0:T(8,128)(2,1)} %get-tuple-element.111.refs_8_) | copy-start | bytes 884740
  126.0 51.0 %collective-permute-start.16 = (bf16[256,4096]{1,0:T(8,128)(2,1)}, bf16[256,4096]{1,0:T(8,128)(2,1)S(1)}, u32[]{:S(2)}, u32[]{:S(2)}) collective-permute-start(bf16[256,4096]{1,0:T(8,128)(2,1)} %collective-permute-done.11.refs_9_.refs_30_), channel_id=1, source_target_pairs={{0,24},{2,26},{4,28},{6,30},{8,0},{10,2},{12,4},{14,6},{16,8},{18,... | collective-permute-start | bytes 6291464 | tf_op jit(solution)/shard_map/ppermute | solution.py:440
  130.0 10.6 %collective-permute-start.12 = (bf16[144,1024]{1,0:T(8,128)(2,1)S(1)}, bf16[144,1024]{1,0:T(8,128)(2,1)S(1)}, u32[]{:S(2)}, u32[]{:S(2)}) collective-permute-start(bf16[144,1024]{1,0:T(8,128)(2,1)S(1)} %copy-done.14), channel_id=1, source_target_pairs={{0,2},{2,0},{4,6},{6,4},{8,10},{10,8},{12,14},{14,12},{16,18},{18,... | collective-permute-start | bytes 884744 | tf_op jit(solution)/shard_map/ppermute | solution.py:429
  131.2 9.5 %collective-permute-start.13 = (bf16[144,1024]{1,0:T(8,128)(2,1)S(1)}, bf16[144,1024]{1,0:T(8,128)(2,1)S(1)}, u32[]{:S(2)}, u32[]{:S(2)}) collective-permute-start(bf16[144,1024]{1,0:T(8,128)(2,1)S(1)} %copy-done.14), channel_id=1, source_target_pairs={{0,4},{2,6},{4,0},{6,2},{8,12},{10,14},{12,8},{14,10},{16,20},{18,... | collective-permute-start | bytes 884744 | tf_op jit(solution)/shard_map/ppermute | solution.py:429
  132.6 11.7 %collective-permute-start.14 = (bf16[144,1024]{1,0:T(8,128)(2,1)S(1)}, bf16[144,1024]{1,0:T(8,128)(2,1)S(1)}, u32[]{:S(2)}, u32[]{:S(2)}) collective-permute-start(bf16[144,1024]{1,0:T(8,128)(2,1)S(1)} %copy-done.14), channel_id=1, source_target_pairs={{0,6},{2,4},{4,2},{6,0},{8,14},{10,12},{12,10},{14,8},{16,22},{18,... | collective-permute-start | bytes 884744 | tf_op jit(solution)/shard_map/ppermute | solution.py:429
  167.3 5.4 %collective-permute-start.15 = (bf16[4,2,256,256]{3,2,1,0:T(8,128)(2,1)}, bf16[4,2,256,256]{3,2,1,0:T(8,128)(2,1)S(1)}, u32[]{:S(2)}, u32[]{:S(2)}) collective-permute-start(bf16[4,2,256,256]{3,2,1,0:T(8,128)(2,1)} %get-tuple-element.118), channel_id=1, source_target_pairs={{0,1},{1,0},{2,3},{3,2},{4,5},{5,4},{6,7},{7,6},{8,9},{9,8},{10,11... | collective-permute-start | bytes 3145736 | tf_op jit(solution)/shard_map/ppermute | solution.py:658
  177.0 9.8 %collective-permute-start.17 = (bf16[256,640]{1,0:T(8,128)(2,1)}, bf16[256,640]{1,0:T(8,128)(2,1)S(1)}, u32[]{:S(2)}, u32[]{:S(2)}) collective-permute-start(bf16[256,640]{1,0:T(8,128)(2,1)} %get-tuple-element.127), channel_id=1, source_target_pairs={{0,2},{2,0},{4,6},{6,4},{8,10},{10,8},{12,14},{14,12},{16,18},{18,... | collective-permute-start | bytes 983048 | tf_op jit(solution)/shard_map/ppermute | solution.py:429
  177.9 8.9 %collective-permute-start.18 = (bf16[256,640]{1,0:T(8,128)(2,1)}, bf16[256,640]{1,0:T(8,128)(2,1)S(1)}, u32[]{:S(2)}, u32[]{:S(2)}) collective-permute-start(bf16[256,640]{1,0:T(8,128)(2,1)} %get-tuple-element.128), channel_id=1, source_target_pairs={{0,4},{2,6},{4,0},{6,2},{8,12},{10,14},{12,8},{14,10},{16,20},{18,... | collective-permute-start | bytes 983048 | tf_op jit(solution)/shard_map/ppermute | solution.py:429
  178.6 15.7 %collective-permute-start.19 = (bf16[256,640]{1,0:T(8,128)(2,1)}, bf16[256,640]{1,0:T(8,128)(2,1)S(1)}, u32[]{:S(2)}, u32[]{:S(2)}) collective-permute-start(bf16[256,640]{1,0:T(8,128)(2,1)} %get-tuple-element.129), channel_id=1, source_target_pairs={{0,6},{2,4},{4,2},{6,0},{8,14},{10,12},{12,10},{14,8},{16,22},{18,... | collective-permute-start | bytes 983048 | tf_op jit(solution)/shard_map/ppermute | solution.py:429
  179.7 7.1 %copy-start.20 = (f32[256,128]{1,0:T(8,128)S(1)}, f32[256,128]{1,0:T(8,128)}, u32[]{:S(2)}) copy-start(f32[256,128]{1,0:T(8,128)} %get-tuple-element.134) | copy-start | bytes 393220
  179.7 14.6 %copy-start.13 = (bf16[256,128]{1,0:T(8,128)(2,1)S(1)}, bf16[256,128]{1,0:T(8,128)(2,1)}, u32[]{:S(2)}) copy-start(bf16[256,128]{1,0:T(8,128)(2,1)} %get-tuple-element.100.refs_8_.refs_2_) | copy-start | bytes 196612
  179.7 14.6 %copy-start.21 = (f32[256,128]{1,0:T(8,128)S(1)}, f32[256,128]{1,0:T(8,128)}, u32[]{:S(2)}) copy-start(f32[256,128]{1,0:T(8,128)} %get-tuple-element.135) | copy-start | bytes 393220
  185.5 10.1 %collective-permute-start.20 = (bf16[1024,256]{1,0:T(8,128)(2,1)S(1)}, bf16[1024,256]{1,0:T(8,128)(2,1)S(1)}, u32[]{:S(2)}, u32[]{:S(2)}) collective-permute-start(bf16[1024,256]{1,0:T(8,128)(2,1)S(1)} %convolution_convert_fusion), channel_id=1, source_target_pairs={{0,1},{2,3},{4,5},{6,7},{9,8},{11,10},{13,12},{15,14},{17,16},{19,... | collective-permute-start | bytes 1572872 | tf_op jit(solution)/shard_map/ppermute | solution.py:675
  194.3 13.7 %copy-start = (bf16[256,640]{1,0:T(8,128)(2,1)S(1)}, bf16[256,640]{1,0:T(8,128)(2,1)}, u32[]{:S(2)}) copy-start(bf16[256,640]{1,0:T(8,128)(2,1)} %get-tuple-element.126.refs_0_) | copy-start | bytes 983044
  194.3 13.7 %copy-start.1 = (s32[3]{0:T(128)S(1)}, s32[3]{0:T(128)}, u32[]{:S(2)}) copy-start(s32[3]{0:T(128)} %pad_add_fusion.at) | copy-start | bytes 40
  194.3 9.8 %collective-permute-start.24 = (f32[2,256,128]{2,1,0:T(8,128)S(1)}, f32[2,256,128]{2,1,0:T(8,128)S(1)}, u32[]{:S(2)}, u32[]{:S(2)}) collective-permute-start(f32[2,256,128]{2,1,0:T(8,128)S(1)} %pad_maximum_fusion), channel_id=1, source_target_pairs={{0,1},{1,0},{2,3},{3,2},{4,5},{5,4},{6,7},{7,6},{8,9},{9,8},{10,11... | collective-permute-start | bytes 786440 | tf_op jit(solution)/shard_map/ppermute | solution.py:707
  195.8 9.2 %collective-permute-start.21 = (bf16[256,256]{1,0:T(8,128)(2,1)S(1)}, bf16[256,256]{1,0:T(8,128)(2,1)S(1)}, u32[]{:S(2)}, u32[]{:S(2)}) collective-permute-start(bf16[256,256]{1,0:T(8,128)(2,1)S(1)} %get-tuple-element.138), channel_id=1, source_target_pairs={{1,3},{3,1},{5,7},{7,5},{8,10},{10,8},{12,14},{14,12},{16,18},{18,... | collective-permute-start | bytes 393224 | tf_op jit(solution)/shard_map/ppermute | solution.py:680
  198.1 6.8 %collective-permute-start.22 = (bf16[256,256]{1,0:T(8,128)(2,1)S(1)}, bf16[256,256]{1,0:T(8,128)(2,1)S(1)}, u32[]{:S(2)}, u32[]{:S(2)}) collective-permute-start(bf16[256,256]{1,0:T(8,128)(2,1)S(1)} %get-tuple-element.137), channel_id=1, source_target_pairs={{1,5},{3,7},{5,1},{7,3},{8,12},{10,14},{12,8},{14,10},{16,20},{18,... | collective-permute-start | bytes 393224 | tf_op jit(solution)/shard_map/ppermute | solution.py:680
  201.4 6.6 %collective-permute-start.23 = (bf16[256,256]{1,0:T(8,128)(2,1)S(1)}, bf16[256,256]{1,0:T(8,128)(2,1)S(1)}, u32[]{:S(2)}, u32[]{:S(2)}) collective-permute-start(bf16[256,256]{1,0:T(8,128)(2,1)S(1)} %get-tuple-element.136), channel_id=1, source_target_pairs={{1,7},{3,5},{5,3},{7,1},{8,14},{10,12},{12,10},{14,8},{16,22},{18,... | collective-permute-start | bytes 393224 | tf_op jit(solution)/shard_map/ppermute | solution.py:680
  (15 other events, 40.9 us)

commit v2 on v0

--- a/solution.py
+++ b/solution.py
@@ -565,6 +565,7 @@
     blocks.append((swap(from_x[:half], 2), swap(from_y[half:], 1)))
     results += [block(j, *blocks[j]) for j in range(1, RING - 1)]
     logs += [v[2] for v in results[1:]]
+    logs, w_blocks[-1] = lax.optimization_barrier((logs, w_blocks[-1]))
     logs, grad_part = lax.optimization_barrier((logs, grad_part))
     grad_parts = [grad_part] + [swap(grad_part, j) for j in range(1, RING)]
 
@@ -591,8 +592,7 @@
         state_part,
     )
 
-    read_parts, w_blocks[-1] = lax.optimization_barrier((read_parts, w_blocks[-1]))
-    after = [read_parts[0]]
+    after = []
     if outer > 2:
         after.append(w_blocks[-1])
     results.append(block(RING - 1, *blocks[-1], after))
@@ -627,6 +627,7 @@
         ]
         + [shape(v, bf16) for v in tile_shapes],
         [pltpu.VMEM((RING * rows, n_w * w_rows), f32)],
+        after=[read_parts[0]],
     )(
         at,
         *local_acts,

time: 206 us -> 209 us (1.015)
  waiting for transfers between devices: 50.4 us -> 54.6 us
    ppermute x3, waiting for transfers between devices: 1.65 us -> 16 us  [turn_w(): w_blocks.append(lax.ppermute(w_blocks[-1], 'seq', turn))]
    ppermute x16, waiting for transfers between devices: 24.2 us -> 14.4 us  [swap(): return lax.ppermute(value, 'seq', [(s, s ^ j) for s in range(n_seq)])]
  transfers between devices with their start and end apart: 28 -> 28, of which waited for: 13 -> 11; matrix products, arithmetic and copies ran while one was open for 3% -> 3% of each run, Pallas kernels for 44% -> 43%
where the time goes in v2:
time: 209 us; the launch traced here: 208 us
  Pallas kernels  91.5 us (44%)
  waiting for transfers between devices  54.6 us (26%)
  starting transfers between devices  44.8 us (21%)
  local copies, waits for them, and re-layouts  7.06 us (3%)
  matrix products  5.79 us (3%)
  other arithmetic  3.2 us (2%)
    pallas_call x12, Pallas kernels, call(): return lambda *operands: fn(*operands, *after)  89.8 us
    ppermute x3, waiting for transfers between devices, turn_w(): w_blocks.append(lax.ppermute(w_blocks[-1], 'seq', turn))  16 us
    ppermute x16, waiting for transfers between devices, swap(): return lax.ppermute(value, 'seq', [(s, s ^ j) for s in range(n_seq)])  14.4 us
    ppermute x1, waiting for transfers between devices, local(): got = lax.ppermute(across, 'seq', [(s, s ^ d * RING) for s in range(n_seq)])  13.4 us
    ppermute x16, starting transfers between devices, swap(): return lax.ppermute(value, 'seq', [(s, s ^ j) for s in range(n_seq)])  13.1 us
    ppermute x3, starting transfers between devices, turn_w(): w_blocks.append(lax.ppermute(w_blocks[-1], 'seq', turn))  12 us
    ppermute x3, starting transfers between devices, local(): lax.ppermute(tile[j], both_axes, [(2 * s + owner(s), 2 * (s ^ j) + owner(...  7.68 us
    ppermute x2, waiting for transfers between devices, along(): lax.ppermute(value, 'seq', [(s, s + d * RING) for s in range(n_seq) if 0...  7.65 us
  transfers between devices with their start and end apart: 28, of which 11 were waited for; matrix products, arithmetic and copies ran while one was open for 3% of the time, Pallas kernels for 43%

profile of v2, /device:TPU:1, one launch (start us, length us, event | category | flops | bytes accessed | tf_op | source)
XLA Modules:
  0.0 207.9 jit_solution(17893808239838544557)
XLA Ops:
  0.6 4.2 %collective-permute-start.10 = (bf16[256,4096]{1,0:T(8,128)(2,1)}, bf16[256,4096]{1,0:T(8,128)(2,1)}, u32[]{:S(2)}, u32[]{:S(2)}) collective-permute-start(bf16[256,4096]{1,0:T(8,128)(2,1)} %refs_28_.1), channel_id=1, source_target_pairs={{0,24},{2,26},{4,28},{6,30},{8,0},{10,2},{12,4},{14,6},{16,8},{18,... | collective-permute-start | bytes 6291464 | tf_op jit(solution)/shard_map/ppermute | solution.py:430
  5.4 8.1 %edges.1 = (bf16[272,1024]{1,0:T(8,128)(2,1)}, bf16[272,1024]{1,0:T(8,128)(2,1)}, bf16[272,1024]{1,0:T(8,128)(2,1)}, bf16[272,1024]{1,0:T(8,128)(2,1)}) custom-call(s32[3]{0:T(128)} %pad_add_fusion.at, bf16[256,4096]{1,0:T(8,128)(2,1)} %refs_31_.1, bf16[256,4096]{1,0:T(8,128)(2,1)} %refs_1_.5, bf16[256,128]{1,0:T(8,128)(2,1)} %refs_2_.5, ...), custom_call_target="tpu_custom_call" | custom-call | tf_op jit(solution)/shard_map/edges/pallas_call | solution.py:399
  16.2 3.8 %pack.1.refs_0_.refs_1_.refs_2_.refs_3_.refs_4_.refs_5_.refs_6_.refs_7_.refs_16_.refs_20_ = bf16[256,4480]{1,0:T(8,128)(2,1)} custom-call(s32[3]{0:T(128)} %pad_add_fusion.at, bf16[256,4096]{1,0:T(8,128)(2,1)} %refs_1_.5, bf16[256,128]{1,0:T(8,128)(2,1)} %refs_2_.5, bf16[256,128]{1,0:T(8,128)(2,1)} %refs_3_.3, f32[32,256]{1,0:T(8,128)} %bitcast.23), custom_call_target="tpu_custom_call" | custom-call | tf_op jit(solution)/shard_map/pack/pallas_call | solution.py:399
  20.0 8.2 %own_tokens.1 = (f32[256,128]{1,0:T(8,128)}, f32[256,128]{1,0:T(8,128)}) custom-call(s32[3]{0:T(128)} %pad_add_fusion.at, bf16[256,4096]{1,0:T(8,128)(2,1)} %refs_31_.1, bf16[256,4096]{1,0:T(8,128)(2,1)} %refs_1_.5, bf16[256,128]{1,0:T(8,128)(2,1)} %refs_2_.5, bf16[256,128]{1,0:T(8,128)(2,1)} %refs_3_.3, f32[32,256]{1,0:T(8,128)} %bitcast.24), custom_call_target="tpu_custom_call" | custom-call | tf_op jit(solution)/shard_map/own_tokens/pallas_call | solution.py:399
  28.2 8.1 %tokens.4 = (bf16[256,4096]{1,0:T(8,128)(2,1)}, bf16[4,128,1024]{2,1,0:T(8,128)(2,1)}, f32[1,4096]{1,0:T(1,128)}, f32[256,128]{1,0:T(8,128)}) custom-call(s32[3]{0:T(128)} %pad_add_fusion.at, bf16[256,4480]{1,0:T(8,128)(2,1)} %pack.1.refs_0_.refs_1_.refs_2_.refs_3_.refs_4_.refs_5_.refs_6_.refs_7_.refs_16_.refs_20_, ...), custom_call_target="tpu_custom_call" | custom-call | tf_op jit(solution)/shard_map/tokens/pallas_call | solution.py:399
  36.3 3.5 %collective-permute-done.2.refs_3_.refs_16_ = bf16[272,1024]{1,0:T(8,128)(2,1)S(1)} collective-permute-done((bf16[272,1024]{1,0:T(8,128)(2,1)}, bf16[272,1024]{1,0:T(8,128)(2,1)S(1)}, u32[]{:S(2)}, u32[]{:S(2)}) %collective-permute-start.2) | collective-permute-done | bytes 557088 | tf_op jit(solution)/shard_map/ppermute | solution.py:419
  42.1 3.4 %messages.1 = (bf16[144,1024]{1,0:T(8,128)(2,1)}, bf16[144,1024]{1,0:T(8,128)(2,1)}) custom-call(s32[3]{0:T(128)} %pad_add_fusion.at, bf16[272,1024]{1,0:T(8,128)(2,1)} %get-tuple-element.75.refs_0_.refs_13_, bf16[272,1024]{1,0:T(8,128)(2,1)} %copy-done.6, bf16[272,1024]{1,0:T(8,128)(2,1)} %copy-done.7, bf16[272,1024]{1,0:T(8,128)(2,1)} %copy-done.8), custom_call_target="tpu_custom_call" | custom-call | tf_op jit(solution)/shard_map/messages/pallas_call | solution.py:399
  48.2 7.6 %collective-permute-done.5.refs_1_.refs_0_ = bf16[144,1024]{1,0:T(8,128)(2,1)S(1)} collective-permute-done((bf16[144,1024]{1,0:T(8,128)(2,1)}, bf16[144,1024]{1,0:T(8,128)(2,1)S(1)}, u32[]{:S(2)}, u32[]{:S(2)}) %collective-permute-start.5) | collective-permute-done | bytes 294944 | tf_op jit(solution)/shard_map/ppermute | solution.py:422
  57.2 2.8 %across.1 = bf16[144,1024]{1,0:T(8,128)(2,1)} custom-call(s32[3]{0:T(128)} %pad_add_fusion.at, bf16[144,1024]{1,0:T(8,128)(2,1)} %get-tuple-element.79.refs_0_, bf16[144,1024]{1,0:T(8,128)(2,1)} %copy-done.9, bf16[144,1024]{1,0:T(8,128)(2,1)} %get-tuple-element.80.refs_2_, bf16[144,1024]{1,0:T(8,128)(2,1)} %copy-done.10), custom_call_target="tpu_custom_call" | custom-call | tf_op jit(solution)/shard_map/across/pallas_call | solution.py:399
  60.1 3.9 %collective-permute-start.7 = (bf16[144,1024]{1,0:T(8,128)(2,1)}, bf16[144,1024]{1,0:T(8,128)(2,1)S(1)}, u32[]{:S(2)}, u32[]{:S(2)}) collective-permute-start(bf16[144,1024]{1,0:T(8,128)(2,1)} %across.1), channel_id=1, source_target_pairs={{0,16},{2,18},{4,20},{6,22},{8,24},{10,26},{12,28},{14,30},{16,0},... | collective-permute-start | bytes 884744 | tf_op jit(solution)/shard_map/ppermute | solution.py:534
  64.0 13.4 %collective-permute-done.7.refs_2_ = bf16[144,1024]{1,0:T(8,128)(2,1)S(1)} collective-permute-done((bf16[144,1024]{1,0:T(8,128)(2,1)}, bf16[144,1024]{1,0:T(8,128)(2,1)S(1)}, u32[]{:S(2)}, u32[]{:S(2)}) %collective-permute-start.7) | collective-permute-done | bytes 294944 | tf_op jit(solution)/shard_map/ppermute | solution.py:534
  77.4 3.8 %collective-permute-start.11 = (bf16[256,4096]{1,0:T(8,128)(2,1)}, bf16[256,4096]{1,0:T(8,128)(2,1)}, u32[]{:S(2)}, u32[]{:S(2)}) collective-permute-start(bf16[256,4096]{1,0:T(8,128)(2,1)} %collective-permute-done.10.refs_29_), channel_id=1, source_target_pairs={{0,24},{2,26},{4,28},{6,30},{8,0},{10,2},{12,4},{14,6},{16,8},{18,... | collective-permute-start | bytes 6291464 | tf_op jit(solution)/shard_map/ppermute | solution.py:430
  81.2 2.7 %settle.1 = (bf16[144,1024]{1,0:T(8,128)(2,1)}, bf16[144,1024]{1,0:T(8,128)(2,1)}) custom-call(s32[3]{0:T(128)} %pad_add_fusion.at, bf16[144,1024]{1,0:T(8,128)(2,1)} %copy-done.9, bf16[144,1024]{1,0:T(8,128)(2,1)} %copy-done.10, bf16[144,1024]{1,0:T(8,128)(2,1)} %copy-done.15), custom_call_target="tpu_custom_call" | custom-call | tf_op jit(solution)/shard_map/settle/pallas_call | solution.py:399
  84.0 6.0 %collective-permute-done.3.refs_0_.refs_1_.refs_2_.refs_3_.refs_4_.refs_5_.refs_6_.refs_7_.refs_17_.refs_21_ = bf16[256,4480]{1,0:T(8,128)(2,1)S(1)} collective-permute-done((bf16[256,4480]{1,0:T(8,128)(2,1)S(1)}, bf16[256,4480]{1,0:T(8,128)(2,1)S(1)}, u32[]{:S(2)}, u32[]{:S(2)}) %collective-permute-start.3) | collective-permute-done | bytes 2293792 | tf_op jit(solution)/shard_map/ppermute | solution.py:419
  93.9 8.0 %tokens.6 = (bf16[256,4096]{1,0:T(8,128)(2,1)}, bf16[4,128,1024]{2,1,0:T(8,128)(2,1)}, f32[1,4096]{1,0:T(1,128)}, f32[256,128]{1,0:T(8,128)}) custom-call(s32[3]{0:T(128)} %pad_add_fusion.at, bf16[256,4480]{1,0:T(8,128)(2,1)} %copy-done.3, bf16[256,4480]{1,0:T(8,128)(2,1)} %copy-done.3, bf16[256,4480]{1,0:T(8,128)(2,1)} %copy-done.3, ...), custom_call_target="tpu_custom_call" | custom-call | tf_op jit(solution)/shard_map/tokens/pallas_call | solution.py:399
  101.9 8.1 %tokens.5 = (bf16[256,4096]{1,0:T(8,128)(2,1)}, bf16[4,128,1024]{2,1,0:T(8,128)(2,1)}, f32[1,4096]{1,0:T(1,128)}, f32[256,128]{1,0:T(8,128)}) custom-call(s32[3]{0:T(128)} %pad_add_fusion.at, bf16[256,4480]{1,0:T(8,128)(2,1)} %copy-done.2, bf16[256,4480]{1,0:T(8,128)(2,1)} %copy-done.2, bf16[256,4480]{1,0:T(8,128)(2,1)} %copy-done.2, ...), custom_call_target="tpu_custom_call" | custom-call | tf_op jit(solution)/shard_map/tokens/pallas_call | solution.py:399
  110.0 16.0 %collective-permute-done.11.refs_8_.refs_30_ = bf16[256,4096]{1,0:T(8,128)(2,1)} collective-permute-done((bf16[256,4096]{1,0:T(8,128)(2,1)}, bf16[256,4096]{1,0:T(8,128)(2,1)}, u32[]{:S(2)}, u32[]{:S(2)}) %collective-permute-start.11) | collective-permute-done | bytes 2097184 | tf_op jit(solution)/shard_map/ppermute | solution.py:430
  126.0 4.0 %collective-permute-start.19 = (bf16[256,4096]{1,0:T(8,128)(2,1)}, bf16[256,4096]{1,0:T(8,128)(2,1)S(1)}, u32[]{:S(2)}, u32[]{:S(2)}) collective-permute-start(bf16[256,4096]{1,0:T(8,128)(2,1)} %collective-permute-done.11.refs_8_.refs_30_), channel_id=1, source_target_pairs={{0,24},{2,26},{4,28},{6,30},{8,0},{10,2},{12,4},{14,6},{16,8},{18,... | collective-permute-start | bytes 6291464 | tf_op jit(solution)/shard_map/ppermute | solution.py:430
  134.0 6.2 %read_carry.1 = (bf16[256,128]{1,0:T(8,128)(2,1)}, bf16[256,128]{1,0:T(8,128)(2,1)}, bf16[256,128]{1,0:T(8,128)(2,1)}, bf16[256,128]{1,0:T(8,128)(2,1)}) custom-call(s32[3]{0:T(128)} %pad_add_fusion.at, bf16[256,4480]{1,0:T(8,128)(2,1)} %pack.1.refs_0_.refs_1_.refs_2_.refs_3_.refs_4_.refs_5_.refs_6_.refs_7_.refs_16_.refs_20_, bf16[256,4480]{1,0:T(8,128)(2,1)} %copy-done.2, ...), custom_call_target="tpu_custom_call" | custom-call | tf_op jit(solution)/shard_map/read_carry/pallas_call | solution.py:399
  140.1 7.9 %tokens.7 = (bf16[256,4096]{1,0:T(8,128)(2,1)}, bf16[4,128,1024]{2,1,0:T(8,128)(2,1)}, f32[1,4096]{1,0:T(1,128)}, f32[256,128]{1,0:T(8,128)}) custom-call(s32[3]{0:T(128)} %pad_add_fusion.at, bf16[128,4480]{1,0:T(8,128)(2,1)} %copy-done.4, bf16[128,4480]{1,0:T(8,128)(2,1)} %copy-done.5, bf16[128,4480]{1,0:T(8,128)(2,1)} %copy-done.4, ...), custom_call_target="tpu_custom_call" | custom-call | tf_op jit(solution)/shard_map/tokens/pallas_call | solution.py:399
  149.0 22.5 %finish.1 = (bf16[1024,4096]{1,0:T(8,128)(2,1)}, bf16[256,4096]{1,0:T(8,128)(2,1)}, f32[256,128]{1,0:T(8,128)}, bf16[4,2,256,256]{3,2,1,0:T(8,128)(2,1)}, bf16[4,2,256,256]{3,2,1,0:T(8,128)(2,1)}) custom-call(s32[3]{0:T(128)} %pad_add_fusion.at, bf16[256,4096]{1,0:T(8,128)(2,1)} %get-tuple-element.65.refs_0_, bf16[256,4096]{1,0:T(8,128)(2,1)} %get-tuple-element.83.refs_1_, ...), custom_call_target="tpu_custom_call" | custom-call | tf_op jit(solution)/shard_map/finish/pallas_call | solution.py:399
  171.5 2.3 %collective-permute-start.15 = (bf16[4,2,256,256]{3,2,1,0:T(8,128)(2,1)}, bf16[4,2,256,256]{3,2,1,0:T(8,128)(2,1)S(1)}, u32[]{:S(2)}, u32[]{:S(2)}) collective-permute-start(bf16[4,2,256,256]{3,2,1,0:T(8,128)(2,1)} %get-tuple-element.112), channel_id=1, source_target_pairs={{0,1},{1,0},{2,3},{3,2},{4,5},{5,4},{6,7},{7,6},{8,9},{9,8},{10,11... | collective-permute-start | bytes 3145736 | tf_op jit(solution)/shard_map/ppermute | solution.py:649
  180.3 5.8 %convolution_convert_fusion = bf16[1024,256]{1,0:T(8,128)(2,1)S(1)} fusion(bf16[1024,4096]{1,0:T(8,128)(2,1)} %get-tuple-element.117, bf16[256,4096]{1,0:T(8,128)(2,1)S(1)} %collective-permute-done.19), kind=kOutput, calls=%fused_computation.1 | convolution fusion | flops 2147745792 | bytes 11010048 | tf_op jit(solution)/shard_map/dot_general | solution.py:20
  187.5 1.9 collective-permute-start.27
  190.1 2.1 %collective-permute-start.22 = (bf16[2,256,256]{2,1,0:T(8,128)(2,1)S(1)}, bf16[2,256,256]{2,1,0:T(8,128)(2,1)S(1)}, u32[]{:S(2)}, u32[]{:S(2)}) collective-permute-start(bf16[2,256,256]{2,1,0:T(8,128)(2,1)S(1)} %get-tuple-element.126), channel_id=1, source_target_pairs={{0,6},{2,4},{4,2},{6,0},{8,14},{10,12},{12,10},{14,8},{16,22},{18,... | collective-permute-start | bytes 786440 | tf_op jit(solution)/shard_map/ppermute | solution.py:419
  192.4 2.2 %collective-permute-start.24 = (bf16[256,256]{1,0:T(8,128)(2,1)S(1)}, bf16[256,256]{1,0:T(8,128)(2,1)S(1)}, u32[]{:S(2)}, u32[]{:S(2)}) collective-permute-start(bf16[256,256]{1,0:T(8,128)(2,1)S(1)} %get-tuple-element.132), channel_id=1, source_target_pairs={{1,3},{3,1},{5,7},{7,5},{8,10},{10,8},{12,14},{14,12},{16,18},{18,... | collective-permute-start | bytes 393224 | tf_op jit(solution)/shard_map/ppermute | solution.py:664
  194.6 2.1 %collective-permute-start.25 = (bf16[256,256]{1,0:T(8,128)(2,1)S(1)}, bf16[256,256]{1,0:T(8,128)(2,1)S(1)}, u32[]{:S(2)}, u32[]{:S(2)}) collective-permute-start(bf16[256,256]{1,0:T(8,128)(2,1)S(1)} %get-tuple-element.131), channel_id=1, source_target_pairs={{1,5},{3,7},{5,1},{7,3},{8,12},{10,14},{12,8},{14,10},{16,20},{18,... | collective-permute-start | bytes 393224 | tf_op jit(solution)/shard_map/ppermute | solution.py:664
  197.5 3.4 %collective-permute-start.26 = (bf16[256,256]{1,0:T(8,128)(2,1)S(1)}, bf16[256,256]{1,0:T(8,128)(2,1)S(1)}, u32[]{:S(2)}, u32[]{:S(2)}) collective-permute-start(bf16[256,256]{1,0:T(8,128)(2,1)S(1)} %get-tuple-element.130), channel_id=1, source_target_pairs={{1,7},{3,5},{5,3},{7,1},{8,14},{10,12},{12,10},{14,8},{16,22},{18,... | collective-permute-start | bytes 393224 | tf_op jit(solution)/shard_map/ppermute | solution.py:664
  201.5 1.5 collective-permute-done.22.refs_3_
  203.1 1.6 collective-permute-done.24.refs_5_
  204.6 1.6 collective-permute-done.25.refs_6_
  206.3 1.7 place.1
  (94 shorter events, 28.4 us)
Async XLA Ops:
  0.6 76.7 %collective-permute-start.10 = (bf16[256,4096]{1,0:T(8,128)(2,1)}, bf16[256,4096]{1,0:T(8,128)(2,1)}, u32[]{:S(2)}, u32[]{:S(2)}) collective-permute-start(bf16[256,4096]{1,0:T(8,128)(2,1)} %refs_28_.1), channel_id=1, source_target_pairs={{0,24},{2,26},{4,28},{6,30},{8,0},{10,2},{12,4},{14,6},{16,8},{18,... | collective-permute-start | bytes 6291464 | tf_op jit(solution)/shard_map/ppermute | solution.py:430
  13.5 22.7 %collective-permute-start = (bf16[272,1024]{1,0:T(8,128)(2,1)}, bf16[272,1024]{1,0:T(8,128)(2,1)S(1)}, u32[]{:S(2)}, u32[]{:S(2)}) collective-permute-start(bf16[272,1024]{1,0:T(8,128)(2,1)} %get-tuple-element.67), channel_id=1, source_target_pairs={{0,2},{2,0},{4,6},{6,4},{8,10},{10,8},{12,14},{14,12},{16,18},{18,... | collective-permute-start | bytes 1671176 | tf_op jit(solution)/shard_map/ppermute | solution.py:419
  14.7 21.6 %collective-permute-start.1 = (bf16[272,1024]{1,0:T(8,128)(2,1)}, bf16[272,1024]{1,0:T(8,128)(2,1)S(1)}, u32[]{:S(2)}, u32[]{:S(2)}) collective-permute-start(bf16[272,1024]{1,0:T(8,128)(2,1)} %get-tuple-element.68), channel_id=1, source_target_pairs={{0,4},{2,6},{4,0},{6,2},{8,12},{10,14},{12,8},{14,10},{16,20},{18,... | collective-permute-start | bytes 1671176 | tf_op jit(solution)/shard_map/ppermute | solution.py:419
  16.0 23.9 %collective-permute-start.2 = (bf16[272,1024]{1,0:T(8,128)(2,1)}, bf16[272,1024]{1,0:T(8,128)(2,1)S(1)}, u32[]{:S(2)}, u32[]{:S(2)}) collective-permute-start(bf16[272,1024]{1,0:T(8,128)(2,1)} %get-tuple-element.69), channel_id=1, source_target_pairs={{0,6},{2,4},{4,2},{6,0},{8,14},{10,12},{12,10},{14,8},{16,22},{18,... | collective-permute-start | bytes 1671176 | tf_op jit(solution)/shard_map/ppermute | solution.py:419
  40.7 49.3 %collective-permute-start.3 = (bf16[256,4480]{1,0:T(8,128)(2,1)S(1)}, bf16[256,4480]{1,0:T(8,128)(2,1)S(1)}, u32[]{:S(2)}, u32[]{:S(2)}) collective-permute-start(bf16[256,4480]{1,0:T(8,128)(2,1)S(1)} %copy-done.1), channel_id=1, source_target_pairs={{0,2},{2,0},{4,6},{6,4},{8,10},{10,8},{12,14},{14,12},{16,18},{18,... | collective-permute-start | bytes 6881288 | tf_op jit(solution)/shard_map/ppermute | solution.py:419
  41.9 49.3 %collective-permute-start.4 = (bf16[256,4480]{1,0:T(8,128)(2,1)S(1)}, bf16[256,4480]{1,0:T(8,128)(2,1)S(1)}, u32[]{:S(2)}, u32[]{:S(2)}) collective-permute-start(bf16[256,4480]{1,0:T(8,128)(2,1)S(1)} %copy-done.1), channel_id=1, source_target_pairs={{0,4},{2,6},{4,0},{6,2},{8,12},{10,14},{12,8},{14,10},{16,20},{18,... | collective-permute-start | bytes 6881288 | tf_op jit(solution)/shard_map/ppermute | solution.py:419
  45.6 10.2 %collective-permute-start.5 = (bf16[144,1024]{1,0:T(8,128)(2,1)}, bf16[144,1024]{1,0:T(8,128)(2,1)S(1)}, u32[]{:S(2)}, u32[]{:S(2)}) collective-permute-start(bf16[144,1024]{1,0:T(8,128)(2,1)} %get-tuple-element.79.refs_0_), channel_id=1, source_target_pairs={{0,8},{2,10},{4,12},{6,14},{8,16},{10,18},{12,20},{14,22},{16,24},... | collective-permute-start | bytes 884744 | tf_op jit(solution)/shard_map/ppermute | solution.py:422
  46.9 8.9 %collective-permute-start.6 = (bf16[144,1024]{1,0:T(8,128)(2,1)}, bf16[144,1024]{1,0:T(8,128)(2,1)S(1)}, u32[]{:S(2)}, u32[]{:S(2)}) collective-permute-start(bf16[144,1024]{1,0:T(8,128)(2,1)} %get-tuple-element.80.refs_2_), channel_id=1, source_target_pairs={{8,0},{10,2},{12,4},{14,6},{16,8},{18,10},{20,12},{22,14},{24,16},... | collective-permute-start | bytes 884744 | tf_op jit(solution)/shard_map/ppermute | solution.py:422
  60.1 17.3 %collective-permute-start.7 = (bf16[144,1024]{1,0:T(8,128)(2,1)}, bf16[144,1024]{1,0:T(8,128)(2,1)S(1)}, u32[]{:S(2)}, u32[]{:S(2)}) collective-permute-start(bf16[144,1024]{1,0:T(8,128)(2,1)} %across.1), channel_id=1, source_target_pairs={{0,16},{2,18},{4,20},{6,22},{8,24},{10,26},{12,28},{14,30},{16,0},... | collective-permute-start | bytes 884744 | tf_op jit(solution)/shard_map/ppermute | solution.py:534
  77.4 48.6 %collective-permute-start.11 = (bf16[256,4096]{1,0:T(8,128)(2,1)}, bf16[256,4096]{1,0:T(8,128)(2,1)}, u32[]{:S(2)}, u32[]{:S(2)}) collective-permute-start(bf16[256,4096]{1,0:T(8,128)(2,1)} %collective-permute-done.10.refs_29_), channel_id=1, source_target_pairs={{0,24},{2,26},{4,28},{6,30},{8,0},{10,2},{12,4},{14,6},{16,8},{18,... | collective-permute-start | bytes 6291464 | tf_op jit(solution)/shard_map/ppermute | solution.py:430
  92.3 40.2 %collective-permute-start.8 = (bf16[128,4480]{1,0:T(8,128)(2,1)}, bf16[128,4480]{1,0:T(8,128)(2,1)S(1)}, u32[]{:S(2)}, u32[]{:S(2)}) collective-permute-start(bf16[128,4480]{1,0:T(8,128)(2,1)} %slice.40), channel_id=1, source_target_pairs={{0,4},{2,6},{4,0},{6,2},{8,12},{10,14},{12,8},{14,10},{16,20},{18,... | collective-permute-start | bytes 3440648 | tf_op jit(solution)/shard_map/ppermute | solution.py:419
  92.9 39.7 %collective-permute-start.9 = (bf16[128,4480]{1,0:T(8,128)(2,1)S(1)}, bf16[128,4480]{1,0:T(8,128)(2,1)S(1)}, u32[]{:S(2)}, u32[]{:S(2)}) collective-permute-start(bf16[128,4480]{1,0:T(8,128)(2,1)S(1)} %slice.41), channel_id=1, source_target_pairs={{0,2},{2,0},{4,6},{6,4},{8,10},{10,8},{12,14},{14,12},{16,18},{18,... | collective-permute-start | bytes 3440648 | tf_op jit(solution)/shard_map/ppermute | solution.py:419
  101.9 28.1 %copy-start.11 = (bf16[144,1024]{1,0:T(8,128)(2,1)S(1)}, bf16[144,1024]{1,0:T(8,128)(2,1)}, u32[]{:S(2)}) copy-start(bf16[144,1024]{1,0:T(8,128)(2,1)} %get-tuple-element.100.refs_8_) | copy-start | bytes 884740
  126.0 54.3 %collective-permute-start.19 = (bf16[256,4096]{1,0:T(8,128)(2,1)}, bf16[256,4096]{1,0:T(8,128)(2,1)S(1)}, u32[]{:S(2)}, u32[]{:S(2)}) collective-permute-start(bf16[256,4096]{1,0:T(8,128)(2,1)} %collective-permute-done.11.refs_8_.refs_30_), channel_id=1, source_target_pairs={{0,24},{2,26},{4,28},{6,30},{8,0},{10,2},{12,4},{14,6},{16,8},{18,... | collective-permute-start | bytes 6291464 | tf_op jit(solution)/shard_map/ppermute | solution.py:430
  130.0 18.0 %collective-permute-start.12 = (bf16[144,1024]{1,0:T(8,128)(2,1)S(1)}, bf16[144,1024]{1,0:T(8,128)(2,1)S(1)}, u32[]{:S(2)}, u32[]{:S(2)}) collective-permute-start(bf16[144,1024]{1,0:T(8,128)(2,1)S(1)} %copy-done.11), channel_id=1, source_target_pairs={{0,2},{2,0},{4,6},{6,4},{8,10},{10,8},{12,14},{14,12},{16,18},{18,... | collective-permute-start | bytes 884744 | tf_op jit(solution)/shard_map/ppermute | solution.py:419
  131.2 16.8 %collective-permute-start.13 = (bf16[144,1024]{1,0:T(8,128)(2,1)S(1)}, bf16[144,1024]{1,0:T(8,128)(2,1)S(1)}, u32[]{:S(2)}, u32[]{:S(2)}) collective-permute-start(bf16[144,1024]{1,0:T(8,128)(2,1)S(1)} %copy-done.11), channel_id=1, source_target_pairs={{0,4},{2,6},{4,0},{6,2},{8,12},{10,14},{12,8},{14,10},{16,20},{18,... | collective-permute-start | bytes 884744 | tf_op jit(solution)/shard_map/ppermute | solution.py:419
  132.5 15.6 %collective-permute-start.14 = (bf16[144,1024]{1,0:T(8,128)(2,1)S(1)}, bf16[144,1024]{1,0:T(8,128)(2,1)S(1)}, u32[]{:S(2)}, u32[]{:S(2)}) collective-permute-start(bf16[144,1024]{1,0:T(8,128)(2,1)S(1)} %copy-done.11), channel_id=1, source_target_pairs={{0,6},{2,4},{4,2},{6,0},{8,14},{10,12},{12,10},{14,8},{16,22},{18,... | collective-permute-start | bytes 884744 | tf_op jit(solution)/shard_map/ppermute | solution.py:419
  149.0 26.0 %copy-start.20 = (bf16[256,128]{1,0:T(8,128)(2,1)S(1)}, bf16[256,128]{1,0:T(8,128)(2,1)}, u32[]{:S(2)}) copy-start(bf16[256,128]{1,0:T(8,128)(2,1)} %get-tuple-element.114) | copy-start | bytes 196612
  149.0 27.3 %copy-start.19 = (bf16[256,128]{1,0:T(8,128)(2,1)S(1)}, bf16[256,128]{1,0:T(8,128)(2,1)}, u32[]{:S(2)}) copy-start(bf16[256,128]{1,0:T(8,128)(2,1)} %get-tuple-element.115) | copy-start | bytes 196612
  149.0 27.4 %copy-start.17 = (f32[256,128]{1,0:T(8,128)S(1)}, f32[256,128]{1,0:T(8,128)}, u32[]{:S(2)}) copy-start(f32[256,128]{1,0:T(8,128)} %get-tuple-element.120) | copy-start | bytes 393220
  171.5 5.9 %collective-permute-start.15 = (bf16[4,2,256,256]{3,2,1,0:T(8,128)(2,1)}, bf16[4,2,256,256]{3,2,1,0:T(8,128)(2,1)S(1)}, u32[]{:S(2)}, u32[]{:S(2)}) collective-permute-start(bf16[4,2,256,256]{3,2,1,0:T(8,128)(2,1)} %get-tuple-element.112), channel_id=1, source_target_pairs={{0,1},{1,0},{2,3},{3,2},{4,5},{5,4},{6,7},{7,6},{8,9},{9,8},{10,11... | collective-permute-start | bytes 3145736 | tf_op jit(solution)/shard_map/ppermute | solution.py:649
  173.8 5.1 %collective-permute-start.16 = (bf16[256,128]{1,0:T(8,128)(2,1)S(1)}, bf16[256,128]{1,0:T(8,128)(2,1)S(1)}, u32[]{:S(2)}, u32[]{:S(2)}) collective-permute-start(bf16[256,128]{1,0:T(8,128)(2,1)S(1)} %copy-done.21), channel_id=1, source_target_pairs={{0,2},{2,0},{4,6},{6,4},{8,10},{10,8},{12,14},{14,12},{16,18},{18,... | collective-permute-start | bytes 196616 | tf_op jit(solution)/shard_map/ppermute | solution.py:419
  175.0 3.9 %collective-permute-start.17 = (bf16[256,128]{1,0:T(8,128)(2,1)S(1)}, bf16[256,128]{1,0:T(8,128)(2,1)S(1)}, u32[]{:S(2)}, u32[]{:S(2)}) collective-permute-start(bf16[256,128]{1,0:T(8,128)(2,1)S(1)} %copy-done.20), channel_id=1, source_target_pairs={{0,4},{2,6},{4,0},{6,2},{8,12},{10,14},{12,8},{14,10},{16,20},{18,... | collective-permute-start | bytes 196616 | tf_op jit(solution)/shard_map/ppermute | solution.py:419
  176.3 4.0 %collective-permute-start.18 = (bf16[256,128]{1,0:T(8,128)(2,1)S(1)}, bf16[256,128]{1,0:T(8,128)(2,1)S(1)}, u32[]{:S(2)}, u32[]{:S(2)}) collective-permute-start(bf16[256,128]{1,0:T(8,128)(2,1)S(1)} %copy-done.19), channel_id=1, source_target_pairs={{0,6},{2,4},{4,2},{6,0},{8,14},{10,12},{12,10},{14,8},{16,22},{18,... | collective-permute-start | bytes 196616 | tf_op jit(solution)/shard_map/ppermute | solution.py:419
  186.1 6.1 %collective-permute-start.23 = (bf16[1024,256]{1,0:T(8,128)(2,1)S(1)}, bf16[1024,256]{1,0:T(8,128)(2,1)S(1)}, u32[]{:S(2)}, u32[]{:S(2)}) collective-permute-start(bf16[1024,256]{1,0:T(8,128)(2,1)S(1)} %convolution_convert_fusion), channel_id=1, source_target_pairs={{0,1},{2,3},{4,5},{6,7},{9,8},{11,10},{13,12},{15,14},{17,16},{19,... | collective-permute-start | bytes 1572872 | tf_op jit(solution)/shard_map/ppermute | solution.py:659
  187.5 4.7 %collective-permute-start.27 = (f32[2,256,128]{2,1,0:T(8,128)S(1)}, f32[2,256,128]{2,1,0:T(8,128)S(1)}, u32[]{:S(2)}, u32[]{:S(2)}) collective-permute-start(f32[2,256,128]{2,1,0:T(8,128)S(1)} %pad_maximum_fusion), channel_id=1, source_target_pairs={{0,1},{1,0},{2,3},{3,2},{4,5},{5,4},{6,7},{7,6},{8,9},{9,8},{10,11... | collective-permute-start | bytes 786440 | tf_op jit(solution)/shard_map/ppermute | solution.py:690
  189.5 8.0 %collective-permute-start.20 = (bf16[2,256,256]{2,1,0:T(8,128)(2,1)S(1)}, bf16[2,256,256]{2,1,0:T(8,128)(2,1)S(1)}, u32[]{:S(2)}, u32[]{:S(2)}) collective-permute-start(bf16[2,256,256]{2,1,0:T(8,128)(2,1)S(1)} %get-tuple-element.128), channel_id=1, source_target_pairs={{0,2},{2,0},{4,6},{6,4},{8,10},{10,8},{12,14},{14,12},{16,18},{18,... | collective-permute-start | bytes 786440 | tf_op jit(solution)/shard_map/ppermute | solution.py:419
  189.8 11.7 %collective-permute-start.21 = (bf16[2,256,256]{2,1,0:T(8,128)(2,1)S(1)}, bf16[2,256,256]{2,1,0:T(8,128)(2,1)S(1)}, u32[]{:S(2)}, u32[]{:S(2)}) collective-permute-start(bf16[2,256,256]{2,1,0:T(8,128)(2,1)S(1)} %get-tuple-element.127), channel_id=1, source_target_pairs={{0,4},{2,6},{4,0},{6,2},{8,12},{10,14},{12,8},{14,10},{16,20},{18,... | collective-permute-start | bytes 786440 | tf_op jit(solution)/shard_map/ppermute | solution.py:419
  190.1 13.0 %collective-permute-start.22 = (bf16[2,256,256]{2,1,0:T(8,128)(2,1)S(1)}, bf16[2,256,256]{2,1,0:T(8,128)(2,1)S(1)}, u32[]{:S(2)}, u32[]{:S(2)}) collective-permute-start(bf16[2,256,256]{2,1,0:T(8,128)(2,1)S(1)} %get-tuple-element.126), channel_id=1, source_target_pairs={{0,6},{2,4},{4,2},{6,0},{8,14},{10,12},{12,10},{14,8},{16,22},{18,... | collective-permute-start | bytes 786440 | tf_op jit(solution)/shard_map/ppermute | solution.py:419
  192.4 12.2 %collective-permute-start.24 = (bf16[256,256]{1,0:T(8,128)(2,1)S(1)}, bf16[256,256]{1,0:T(8,128)(2,1)S(1)}, u32[]{:S(2)}, u32[]{:S(2)}) collective-permute-start(bf16[256,256]{1,0:T(8,128)(2,1)S(1)} %get-tuple-element.132), channel_id=1, source_target_pairs={{1,3},{3,1},{5,7},{7,5},{8,10},{10,8},{12,14},{14,12},{16,18},{18,... | collective-permute-start | bytes 393224 | tf_op jit(solution)/shard_map/ppermute | solution.py:664
  194.6 11.7 %collective-permute-start.25 = (bf16[256,256]{1,0:T(8,128)(2,1)S(1)}, bf16[256,256]{1,0:T(8,128)(2,1)S(1)}, u32[]{:S(2)}, u32[]{:S(2)}) collective-permute-start(bf16[256,256]{1,0:T(8,128)(2,1)S(1)} %get-tuple-element.131), channel_id=1, source_target_pairs={{1,5},{3,7},{5,1},{7,3},{8,12},{10,14},{12,8},{14,10},{16,20},{18,... | collective-permute-start | bytes 393224 | tf_op jit(solution)/shard_map/ppermute | solution.py:664
  197.5 8.8 %collective-permute-start.26 = (bf16[256,256]{1,0:T(8,128)(2,1)S(1)}, bf16[256,256]{1,0:T(8,128)(2,1)S(1)}, u32[]{:S(2)}, u32[]{:S(2)}) collective-permute-start(bf16[256,256]{1,0:T(8,128)(2,1)S(1)} %get-tuple-element.130), channel_id=1, source_target_pairs={{1,7},{3,5},{5,3},{7,1},{8,14},{10,12},{12,10},{14,8},{16,22},{18,... | collective-permute-start | bytes 393224 | tf_op jit(solution)/shard_map/ppermute | solution.py:664
  (18 other events, 94.9 us)

commit v3 on v1

--- a/solution.py
+++ b/solution.py
@@ -684,7 +684,7 @@
             )
             for j in range(1, RING)
         ]
-        early = to_owners(early)
+        early, late = lax.optimization_barrier((to_owners(early), late))
         read_got = [v[:, share * w_rows :] for v in early[1:]]
         input_grad = pl.pallas_call(
             functools.partial(place_kernel, outer, share),

time: 211 us -> 209 us (level)
    ppermute x13, waiting for transfers between devices: 28.8 us -> 26.4 us  [swap(): return lax.ppermute(value, 'seq', [(s, s ^ j) for s in range(n_seq)])]
    unnamed x44 -> x50, local copies, waits for them, and re-layouts: 5.42 us -> 5.38 us
  transfers between devices with their start and end apart: 25 -> 25, of which waited for: 12 -> 14; matrix products, arithmetic and copies ran while one was open for 4% -> 1% of each run, Pallas kernels for 44% -> 46%
where the time goes in v3:
time: 209 us; the launch traced here: 207 us
  Pallas kernels  94.6 us (45%)
  waiting for transfers between devices  55.8 us (27%)
  starting transfers between devices  41.8 us (20%)
  local copies, waits for them, and re-layouts  7.45 us (4%)
  matrix products  5.83 us (3%)
    pallas_call x13, Pallas kernels, call(): return lambda *operands: fn(*operands, *after)  93 us
    ppermute x13, waiting for transfers between devices, swap(): return lax.ppermute(value, 'seq', [(s, s ^ j) for s in range(n_seq)])  26.4 us
    ppermute x1, waiting for transfers between devices, local(): got = lax.ppermute(across, 'seq', [(s, s ^ d * RING) for s in range(n_seq)])  13.4 us
    ppermute x3, starting transfers between devices, turn_w(): w_blocks.append(lax.ppermute(w_blocks[-1], 'seq', turn))  12 us
    ppermute x13, starting transfers between devices, swap(): return lax.ppermute(value, 'seq', [(s, s ^ j) for s in range(n_seq)])  10.5 us
    ppermute x3, starting transfers between devices, local(): lax.ppermute(tile[j], both_axes, [(2 * s + owner(s), 2 * (s ^ j) + owner(...  8.37 us
    ppermute x2, waiting for transfers between devices, along(): lax.ppermute(value, 'seq', [(s, s + d * RING) for s in range(n_seq) if 0...  7.65 us
    dot_general x1, matrix products, mm(): return lax.dot_general(a, b, dims, preferred_element_type=f32)  5.83 us
  transfers between devices with their start and end apart: 25, of which 14 were waited for; matrix products, arithmetic and copies ran while one was open for 1% of the time, Pallas kernels for 46%

profile of v3, /device:TPU:1, one launch (start us, length us, event | category | flops | bytes accessed | tf_op | source)
XLA Modules:
  0.0 207.3 jit_solution(12306707703416060521)
XLA Ops:
  0.6 4.2 %collective-permute-start.10 = (bf16[256,4096]{1,0:T(8,128)(2,1)}, bf16[256,4096]{1,0:T(8,128)(2,1)}, u32[]{:S(2)}, u32[]{:S(2)}) collective-permute-start(bf16[256,4096]{1,0:T(8,128)(2,1)} %refs_28_.1), channel_id=1, source_target_pairs={{0,24},{2,26},{4,28},{6,30},{8,0},{10,2},{12,4},{14,6},{16,8},{18,... | collective-permute-start | bytes 6291464 | tf_op jit(solution)/shard_map/ppermute | solution.py:440
  5.4 8.1 %edges.1 = (bf16[272,1024]{1,0:T(8,128)(2,1)}, bf16[272,1024]{1,0:T(8,128)(2,1)}, bf16[272,1024]{1,0:T(8,128)(2,1)}, bf16[272,1024]{1,0:T(8,128)(2,1)}) custom-call(s32[3]{0:T(128)} %pad_add_fusion.at, bf16[256,4096]{1,0:T(8,128)(2,1)} %refs_31_.1, bf16[256,4096]{1,0:T(8,128)(2,1)} %refs_1_.5, bf16[256,128]{1,0:T(8,128)(2,1)} %refs_2_.5, ...), custom_call_target="tpu_custom_call" | custom-call | tf_op jit(solution)/shard_map/edges/pallas_call | solution.py:409
  16.2 3.8 %pack.1.refs_0_.refs_1_.refs_2_.refs_3_.refs_4_.refs_5_.refs_6_.refs_7_.refs_16_.refs_20_ = bf16[256,4480]{1,0:T(8,128)(2,1)} custom-call(s32[3]{0:T(128)} %pad_add_fusion.at, bf16[256,4096]{1,0:T(8,128)(2,1)} %refs_1_.5, bf16[256,128]{1,0:T(8,128)(2,1)} %refs_2_.5, bf16[256,128]{1,0:T(8,128)(2,1)} %refs_3_.3, f32[32,256]{1,0:T(8,128)} %bitcast.15), custom_call_target="tpu_custom_call" | custom-call | tf_op jit(solution)/shard_map/pack/pallas_call | solution.py:409
  20.0 8.2 %own_tokens.1 = (f32[256,128]{1,0:T(8,128)}, f32[256,128]{1,0:T(8,128)}) custom-call(s32[3]{0:T(128)} %pad_add_fusion.at, bf16[256,4096]{1,0:T(8,128)(2,1)} %refs_31_.1, bf16[256,4096]{1,0:T(8,128)(2,1)} %refs_1_.5, bf16[256,128]{1,0:T(8,128)(2,1)} %refs_2_.5, bf16[256,128]{1,0:T(8,128)(2,1)} %refs_3_.3, f32[32,256]{1,0:T(8,128)} %bitcast.16), custom_call_target="tpu_custom_call" | custom-call | tf_op jit(solution)/shard_map/own_tokens/pallas_call | solution.py:409
  28.2 8.1 %tokens.4 = (bf16[256,4096]{1,0:T(8,128)(2,1)}, bf16[4,128,1024]{2,1,0:T(8,128)(2,1)}, f32[1,4096]{1,0:T(1,128)}, f32[256,128]{1,0:T(8,128)}) custom-call(s32[3]{0:T(128)} %pad_add_fusion.at, bf16[256,4480]{1,0:T(8,128)(2,1)} %pack.1.refs_0_.refs_1_.refs_2_.refs_3_.refs_4_.refs_5_.refs_6_.refs_7_.refs_16_.refs_20_, ...), custom_call_target="tpu_custom_call" | custom-call | tf_op jit(solution)/shard_map/tokens/pallas_call | solution.py:409
  36.3 3.5 %collective-permute-done.2.refs_3_.refs_16_ = bf16[272,1024]{1,0:T(8,128)(2,1)S(1)} collective-permute-done((bf16[272,1024]{1,0:T(8,128)(2,1)}, bf16[272,1024]{1,0:T(8,128)(2,1)S(1)}, u32[]{:S(2)}, u32[]{:S(2)}) %collective-permute-start.2) | collective-permute-done | bytes 557088 | tf_op jit(solution)/shard_map/ppermute | solution.py:429
  42.1 3.4 %messages.1 = (bf16[144,1024]{1,0:T(8,128)(2,1)}, bf16[144,1024]{1,0:T(8,128)(2,1)}) custom-call(s32[3]{0:T(128)} %pad_add_fusion.at, bf16[272,1024]{1,0:T(8,128)(2,1)} %get-tuple-element.88.refs_0_.refs_13_, bf16[272,1024]{1,0:T(8,128)(2,1)} %copy-done.7, bf16[272,1024]{1,0:T(8,128)(2,1)} %copy-done.8, bf16[272,1024]{1,0:T(8,128)(2,1)} %copy-done.9), custom_call_target="tpu_custom_call" | custom-call | tf_op jit(solution)/shard_map/messages/pallas_call | solution.py:409
  48.2 7.6 %collective-permute-done.5.refs_1_.refs_0_ = bf16[144,1024]{1,0:T(8,128)(2,1)S(1)} collective-permute-done((bf16[144,1024]{1,0:T(8,128)(2,1)}, bf16[144,1024]{1,0:T(8,128)(2,1)S(1)}, u32[]{:S(2)}, u32[]{:S(2)}) %collective-permute-start.5) | collective-permute-done | bytes 294944 | tf_op jit(solution)/shard_map/ppermute | solution.py:432
  57.2 2.8 %across.1 = bf16[144,1024]{1,0:T(8,128)(2,1)} custom-call(s32[3]{0:T(128)} %pad_add_fusion.at, bf16[144,1024]{1,0:T(8,128)(2,1)} %get-tuple-element.92.refs_0_, bf16[144,1024]{1,0:T(8,128)(2,1)} %copy-done.10, bf16[144,1024]{1,0:T(8,128)(2,1)} %get-tuple-element.93.refs_2_, bf16[144,1024]{1,0:T(8,128)(2,1)} %copy-done.11), custom_call_target="tpu_custom_call" | custom-call | tf_op jit(solution)/shard_map/across/pallas_call | solution.py:409
  60.1 3.9 %collective-permute-start.7 = (bf16[144,1024]{1,0:T(8,128)(2,1)}, bf16[144,1024]{1,0:T(8,128)(2,1)S(1)}, u32[]{:S(2)}, u32[]{:S(2)}) collective-permute-start(bf16[144,1024]{1,0:T(8,128)(2,1)} %across.1), channel_id=1, source_target_pairs={{0,16},{2,18},{4,20},{6,22},{8,24},{10,26},{12,28},{14,30},{16,0},... | collective-permute-start | bytes 884744 | tf_op jit(solution)/shard_map/ppermute | solution.py:544
  64.0 13.4 %collective-permute-done.7.refs_2_ = bf16[144,1024]{1,0:T(8,128)(2,1)S(1)} collective-permute-done((bf16[144,1024]{1,0:T(8,128)(2,1)}, bf16[144,1024]{1,0:T(8,128)(2,1)S(1)}, u32[]{:S(2)}, u32[]{:S(2)}) %collective-permute-start.7) | collective-permute-done | bytes 294944 | tf_op jit(solution)/shard_map/ppermute | solution.py:544
  77.4 3.8 %collective-permute-start.11 = (bf16[256,4096]{1,0:T(8,128)(2,1)}, bf16[256,4096]{1,0:T(8,128)(2,1)}, u32[]{:S(2)}, u32[]{:S(2)}) collective-permute-start(bf16[256,4096]{1,0:T(8,128)(2,1)} %collective-permute-done.10.refs_29_), channel_id=1, source_target_pairs={{0,24},{2,26},{4,28},{6,30},{8,0},{10,2},{12,4},{14,6},{16,8},{18,... | collective-permute-start | bytes 6291464 | tf_op jit(solution)/shard_map/ppermute | solution.py:440
  81.2 2.7 %settle.1 = (bf16[144,1024]{1,0:T(8,128)(2,1)}, bf16[144,1024]{1,0:T(8,128)(2,1)}) custom-call(s32[3]{0:T(128)} %pad_add_fusion.at, bf16[144,1024]{1,0:T(8,128)(2,1)} %copy-done.10, bf16[144,1024]{1,0:T(8,128)(2,1)} %copy-done.11, bf16[144,1024]{1,0:T(8,128)(2,1)} %copy-done.18), custom_call_target="tpu_custom_call" | custom-call | tf_op jit(solution)/shard_map/settle/pallas_call | solution.py:409
  84.0 6.0 %collective-permute-done.3.refs_0_.refs_1_.refs_2_.refs_3_.refs_4_.refs_5_.refs_6_.refs_7_.refs_17_.refs_21_ = bf16[256,4480]{1,0:T(8,128)(2,1)S(1)} collective-permute-done((bf16[256,4480]{1,0:T(8,128)(2,1)S(1)}, bf16[256,4480]{1,0:T(8,128)(2,1)S(1)}, u32[]{:S(2)}, u32[]{:S(2)}) %collective-permute-start.3) | collective-permute-done | bytes 2293792 | tf_op jit(solution)/shard_map/ppermute | solution.py:429
  93.9 8.0 %tokens.6 = (bf16[256,4096]{1,0:T(8,128)(2,1)}, bf16[4,128,1024]{2,1,0:T(8,128)(2,1)}, f32[1,4096]{1,0:T(1,128)}, f32[256,128]{1,0:T(8,128)}) custom-call(s32[3]{0:T(128)} %pad_add_fusion.at, bf16[256,4480]{1,0:T(8,128)(2,1)} %copy-done.4, bf16[256,4480]{1,0:T(8,128)(2,1)} %copy-done.4, bf16[256,4480]{1,0:T(8,128)(2,1)} %copy-done.4, ...), custom_call_target="tpu_custom_call" | custom-call | tf_op jit(solution)/shard_map/tokens/pallas_call | solution.py:409
  101.9 8.0 %tokens.5 = (bf16[256,4096]{1,0:T(8,128)(2,1)}, bf16[4,128,1024]{2,1,0:T(8,128)(2,1)}, f32[1,4096]{1,0:T(1,128)}, f32[256,128]{1,0:T(8,128)}) custom-call(s32[3]{0:T(128)} %pad_add_fusion.at, bf16[256,4480]{1,0:T(8,128)(2,1)} %copy-done.3, bf16[256,4480]{1,0:T(8,128)(2,1)} %copy-done.3, bf16[256,4480]{1,0:T(8,128)(2,1)} %copy-done.3, ...), custom_call_target="tpu_custom_call" | custom-call | tf_op jit(solution)/shard_map/tokens/pallas_call | solution.py:409
  109.8 5.4 %collective-permute-done.8.refs_3_.refs_11_.refs_0_.refs_2_.refs_4_.refs_6_.refs_19_ = bf16[128,4480]{1,0:T(8,128)(2,1)S(1)} collective-permute-done((bf16[128,4480]{1,0:T(8,128)(2,1)S(1)}, bf16[128,4480]{1,0:T(8,128)(2,1)S(1)}, u32[]{:S(2)}, u32[]{:S(2)}) %collective-permute-start.8) | collective-permute-done | bytes 1146912 | tf_op jit(solution)/shard_map/ppermute | solution.py:429
  115.2 1.9 collective-permute-done.9.refs_7_.refs_12_.refs_1_.refs_3_.refs_5_.refs_23_
  118.1 6.3 %read_carry.1 = (bf16[256,128]{1,0:T(8,128)(2,1)}, bf16[256,128]{1,0:T(8,128)(2,1)}, bf16[256,128]{1,0:T(8,128)(2,1)}, bf16[256,128]{1,0:T(8,128)(2,1)}) custom-call(s32[3]{0:T(128)} %pad_add_fusion.at, bf16[256,4480]{1,0:T(8,128)(2,1)} %pack.1.refs_0_.refs_1_.refs_2_.refs_3_.refs_4_.refs_5_.refs_6_.refs_7_.refs_16_.refs_20_, bf16[256,4480]{1,0:T(8,128)(2,1)} %copy-done.3, ...), custom_call_target="tpu_custom_call" | custom-call | tf_op jit(solution)/shard_map/read_carry/pallas_call | solution.py:409
  126.0 4.0 %collective-permute-start.16 = (bf16[256,4096]{1,0:T(8,128)(2,1)}, bf16[256,4096]{1,0:T(8,128)(2,1)S(1)}, u32[]{:S(2)}, u32[]{:S(2)}) collective-permute-start(bf16[256,4096]{1,0:T(8,128)(2,1)} %collective-permute-done.11.refs_9_.refs_30_), channel_id=1, source_target_pairs={{0,24},{2,26},{4,28},{6,30},{8,0},{10,2},{12,4},{14,6},{16,8},{18,... | collective-permute-start | bytes 6291464 | tf_op jit(solution)/shard_map/ppermute | solution.py:440
  132.7 7.9 %tokens.7 = (bf16[256,4096]{1,0:T(8,128)(2,1)}, bf16[4,128,1024]{2,1,0:T(8,128)(2,1)}, f32[1,4096]{1,0:T(1,128)}, f32[256,128]{1,0:T(8,128)}) custom-call(s32[3]{0:T(128)} %pad_add_fusion.at, bf16[128,4480]{1,0:T(8,128)(2,1)} %copy-done.5, bf16[128,4480]{1,0:T(8,128)(2,1)} %copy-done.6, bf16[128,4480]{1,0:T(8,128)(2,1)} %copy-done.5, ...), custom_call_target="tpu_custom_call" | custom-call | tf_op jit(solution)/shard_map/tokens/pallas_call | solution.py:409
  140.6 3.7 %collective-permute-done.14.refs_11_ = bf16[144,1024]{1,0:T(8,128)(2,1)S(1)} collective-permute-done((bf16[144,1024]{1,0:T(8,128)(2,1)S(1)}, bf16[144,1024]{1,0:T(8,128)(2,1)S(1)}, u32[]{:S(2)}, u32[]{:S(2)}) %collective-permute-start.14) | collective-permute-done | bytes 294944 | tf_op jit(solution)/shard_map/ppermute | solution.py:429
  145.0 22.3 %finish.1 = (bf16[1024,4096]{1,0:T(8,128)(2,1)}, bf16[256,4096]{1,0:T(8,128)(2,1)}, f32[256,128]{1,0:T(8,128)}, bf16[4,2,256,256]{3,2,1,0:T(8,128)(2,1)}, bf16[4,2,256,256]{3,2,1,0:T(8,128)(2,1)}) custom-call(s32[3]{0:T(128)} %pad_add_fusion.at, bf16[256,4096]{1,0:T(8,128)(2,1)} %get-tuple-element.78.refs_0_, bf16[256,4096]{1,0:T(8,128)(2,1)} %get-tuple-element.96.refs_1_, ...), custom_call_target="tpu_custom_call" | custom-call | tf_op jit(solution)/shard_map/finish/pallas_call | solution.py:409
  167.3 2.9 %collective-permute-start.15 = (bf16[4,2,256,256]{3,2,1,0:T(8,128)(2,1)}, bf16[4,2,256,256]{3,2,1,0:T(8,128)(2,1)S(1)}, u32[]{:S(2)}, u32[]{:S(2)}) collective-permute-start(bf16[4,2,256,256]{3,2,1,0:T(8,128)(2,1)} %get-tuple-element.126), channel_id=1, source_target_pairs={{0,1},{1,0},{2,3},{3,2},{4,5},{5,4},{6,7},{7,6},{8,9},{9,8},{10,11... | collective-permute-start | bytes 3145736 | tf_op jit(solution)/shard_map/ppermute | solution.py:658
  170.2 2.5 %collective-permute-done.15.refs_1_ = bf16[4,2,256,256]{3,2,1,0:T(8,128)(2,1)S(1)} collective-permute-done((bf16[4,2,256,256]{3,2,1,0:T(8,128)(2,1)}, bf16[4,2,256,256]{3,2,1,0:T(8,128)(2,1)S(1)}, u32[]{:S(2)}, u32[]{:S(2)}) %collective-permute-start.15) | collective-permute-done | bytes 1048608 | tf_op jit(solution)/shard_map/ppermute | solution.py:658
  173.6 3.3 %early_sums.1 = (bf16[256,640]{1,0:T(8,128)(2,1)}, bf16[256,640]{1,0:T(8,128)(2,1)}, bf16[256,640]{1,0:T(8,128)(2,1)}, bf16[256,640]{1,0:T(8,128)(2,1)}) custom-call(s32[3]{0:T(128)} %pad_add_fusion.at, bf16[4,2,256,256]{3,2,1,0:T(8,128)(2,1)} %get-tuple-element.125.refs_0_, bf16[4,2,256,256]{3,2,1,0:T(8,128)(2,1)} %copy-done.12, ...), custom_call_target="tpu_custom_call" | custom-call | tf_op jit(solution)/shard_map/early_sums/pallas_call | solution.py:409
  177.0 5.8 %convolution_convert_fusion = bf16[1024,256]{1,0:T(8,128)(2,1)S(1)} fusion(bf16[1024,4096]{1,0:T(8,128)(2,1)} %get-tuple-element.138, bf16[256,4096]{1,0:T(8,128)(2,1)S(1)} %collective-permute-done.16), kind=kOutput, calls=%fused_computation | convolution fusion | flops 2147745792 | bytes 11010048 | tf_op jit(solution)/shard_map/dot_general | solution.py:20
  187.3 2.8 %collective-permute-start.21 = (bf16[256,256]{1,0:T(8,128)(2,1)S(1)}, bf16[256,256]{1,0:T(8,128)(2,1)S(1)}, u32[]{:S(2)}, u32[]{:S(2)}) collective-permute-start(bf16[256,256]{1,0:T(8,128)(2,1)S(1)} %get-tuple-element.154), channel_id=1, source_target_pairs={{1,3},{3,1},{5,7},{7,5},{8,10},{10,8},{12,14},{14,12},{16,18},{18,... | collective-permute-start | bytes 393224 | tf_op jit(solution)/shard_map/ppermute | solution.py:680
  190.0 2.6 %collective-permute-start.22 = (bf16[256,256]{1,0:T(8,128)(2,1)S(1)}, bf16[256,256]{1,0:T(8,128)(2,1)S(1)}, u32[]{:S(2)}, u32[]{:S(2)}) collective-permute-start(bf16[256,256]{1,0:T(8,128)(2,1)S(1)} %get-tuple-element.153), channel_id=1, source_target_pairs={{1,5},{3,7},{5,1},{7,3},{8,12},{10,14},{12,8},{14,10},{16,20},{18,... | collective-permute-start | bytes 393224 | tf_op jit(solution)/shard_map/ppermute | solution.py:680
  192.7 3.0 %collective-permute-start.23 = (bf16[256,256]{1,0:T(8,128)(2,1)S(1)}, bf16[256,256]{1,0:T(8,128)(2,1)S(1)}, u32[]{:S(2)}, u32[]{:S(2)}) collective-permute-start(bf16[256,256]{1,0:T(8,128)(2,1)S(1)} %get-tuple-element.152), channel_id=1, source_target_pairs={{1,7},{3,5},{5,3},{7,1},{8,14},{10,12},{12,10},{14,8},{16,22},{18,... | collective-permute-start | bytes 393224 | tf_op jit(solution)/shard_map/ppermute | solution.py:680
  195.7 4.8 %collective-permute-done.19.refs_3_ = bf16[256,640]{1,0:T(8,128)(2,1)S(1)} collective-permute-done((bf16[256,640]{1,0:T(8,128)(2,1)S(1)}, bf16[256,640]{1,0:T(8,128)(2,1)S(1)}, u32[]{:S(2)}, u32[]{:S(2)}) %collective-permute-start.19) | collective-permute-done | bytes 327712 | tf_op jit(solution)/shard_map/ppermute | solution.py:429
  200.5 1.8 collective-permute-done.21.refs_5_
  (93 shorter events, 29.7 us)
Async XLA Ops:
  0.6 76.7 %collective-permute-start.10 = (bf16[256,4096]{1,0:T(8,128)(2,1)}, bf16[256,4096]{1,0:T(8,128)(2,1)}, u32[]{:S(2)}, u32[]{:S(2)}) collective-permute-start(bf16[256,4096]{1,0:T(8,128)(2,1)} %refs_28_.1), channel_id=1, source_target_pairs={{0,24},{2,26},{4,28},{6,30},{8,0},{10,2},{12,4},{14,6},{16,8},{18,... | collective-permute-start | bytes 6291464 | tf_op jit(solution)/shard_map/ppermute | solution.py:440
  13.5 22.7 %collective-permute-start = (bf16[272,1024]{1,0:T(8,128)(2,1)}, bf16[272,1024]{1,0:T(8,128)(2,1)S(1)}, u32[]{:S(2)}, u32[]{:S(2)}) collective-permute-start(bf16[272,1024]{1,0:T(8,128)(2,1)} %get-tuple-element.80), channel_id=1, source_target_pairs={{0,2},{2,0},{4,6},{6,4},{8,10},{10,8},{12,14},{14,12},{16,18},{18,... | collective-permute-start | bytes 1671176 | tf_op jit(solution)/shard_map/ppermute | solution.py:429
  14.7 21.6 %collective-permute-start.1 = (bf16[272,1024]{1,0:T(8,128)(2,1)}, bf16[272,1024]{1,0:T(8,128)(2,1)S(1)}, u32[]{:S(2)}, u32[]{:S(2)}) collective-permute-start(bf16[272,1024]{1,0:T(8,128)(2,1)} %get-tuple-element.81), channel_id=1, source_target_pairs={{0,4},{2,6},{4,0},{6,2},{8,12},{10,14},{12,8},{14,10},{16,20},{18,... | collective-permute-start | bytes 1671176 | tf_op jit(solution)/shard_map/ppermute | solution.py:429
  16.0 23.9 %collective-permute-start.2 = (bf16[272,1024]{1,0:T(8,128)(2,1)}, bf16[272,1024]{1,0:T(8,128)(2,1)S(1)}, u32[]{:S(2)}, u32[]{:S(2)}) collective-permute-start(bf16[272,1024]{1,0:T(8,128)(2,1)} %get-tuple-element.82), channel_id=1, source_target_pairs={{0,6},{2,4},{4,2},{6,0},{8,14},{10,12},{12,10},{14,8},{16,22},{18,... | collective-permute-start | bytes 1671176 | tf_op jit(solution)/shard_map/ppermute | solution.py:429
  28.2 12.5 %copy-start.2 = (bf16[256,4480]{1,0:T(8,128)(2,1)S(1)}, bf16[256,4480]{1,0:T(8,128)(2,1)}, u32[]{:S(2)}) copy-start(bf16[256,4480]{1,0:T(8,128)(2,1)} %pack.1.refs_0_.refs_1_.refs_2_.refs_3_.refs_4_.refs_5_.refs_6_.refs_7_.refs_16_.refs_20_) | copy-start | bytes 6881284
  40.7 49.3 %collective-permute-start.3 = (bf16[256,4480]{1,0:T(8,128)(2,1)S(1)}, bf16[256,4480]{1,0:T(8,128)(2,1)S(1)}, u32[]{:S(2)}, u32[]{:S(2)}) collective-permute-start(bf16[256,4480]{1,0:T(8,128)(2,1)S(1)} %copy-done.2), channel_id=1, source_target_pairs={{0,2},{2,0},{4,6},{6,4},{8,10},{10,8},{12,14},{14,12},{16,18},{18,... | collective-permute-start | bytes 6881288 | tf_op jit(solution)/shard_map/ppermute | solution.py:429
  41.9 49.3 %collective-permute-start.4 = (bf16[256,4480]{1,0:T(8,128)(2,1)S(1)}, bf16[256,4480]{1,0:T(8,128)(2,1)S(1)}, u32[]{:S(2)}, u32[]{:S(2)}) collective-permute-start(bf16[256,4480]{1,0:T(8,128)(2,1)S(1)} %copy-done.2), channel_id=1, source_target_pairs={{0,4},{2,6},{4,0},{6,2},{8,12},{10,14},{12,8},{14,10},{16,20},{18,... | collective-permute-start | bytes 6881288 | tf_op jit(solution)/shard_map/ppermute | solution.py:429
  45.6 10.2 %collective-permute-start.5 = (bf16[144,1024]{1,0:T(8,128)(2,1)}, bf16[144,1024]{1,0:T(8,128)(2,1)S(1)}, u32[]{:S(2)}, u32[]{:S(2)}) collective-permute-start(bf16[144,1024]{1,0:T(8,128)(2,1)} %get-tuple-element.92.refs_0_), channel_id=1, source_target_pairs={{0,8},{2,10},{4,12},{6,14},{8,16},{10,18},{12,20},{14,22},{16,24},... | collective-permute-start | bytes 884744 | tf_op jit(solution)/shard_map/ppermute | solution.py:432
  46.9 8.9 %collective-permute-start.6 = (bf16[144,1024]{1,0:T(8,128)(2,1)}, bf16[144,1024]{1,0:T(8,128)(2,1)S(1)}, u32[]{:S(2)}, u32[]{:S(2)}) collective-permute-start(bf16[144,1024]{1,0:T(8,128)(2,1)} %get-tuple-element.93.refs_2_), channel_id=1, source_target_pairs={{8,0},{10,2},{12,4},{14,6},{16,8},{18,10},{20,12},{22,14},{24,16},... | collective-permute-start | bytes 884744 | tf_op jit(solution)/shard_map/ppermute | solution.py:432
  60.1 17.3 %collective-permute-start.7 = (bf16[144,1024]{1,0:T(8,128)(2,1)}, bf16[144,1024]{1,0:T(8,128)(2,1)S(1)}, u32[]{:S(2)}, u32[]{:S(2)}) collective-permute-start(bf16[144,1024]{1,0:T(8,128)(2,1)} %across.1), channel_id=1, source_target_pairs={{0,16},{2,18},{4,20},{6,22},{8,24},{10,26},{12,28},{14,30},{16,0},... | collective-permute-start | bytes 884744 | tf_op jit(solution)/shard_map/ppermute | solution.py:544
  77.4 48.6 %collective-permute-start.11 = (bf16[256,4096]{1,0:T(8,128)(2,1)}, bf16[256,4096]{1,0:T(8,128)(2,1)}, u32[]{:S(2)}, u32[]{:S(2)}) collective-permute-start(bf16[256,4096]{1,0:T(8,128)(2,1)} %collective-permute-done.10.refs_29_), channel_id=1, source_target_pairs={{0,24},{2,26},{4,28},{6,30},{8,0},{10,2},{12,4},{14,6},{16,8},{18,... | collective-permute-start | bytes 6291464 | tf_op jit(solution)/shard_map/ppermute | solution.py:440
  91.2 24.0 %collective-permute-start.8 = (bf16[128,4480]{1,0:T(8,128)(2,1)S(1)}, bf16[128,4480]{1,0:T(8,128)(2,1)S(1)}, u32[]{:S(2)}, u32[]{:S(2)}) collective-permute-start(bf16[128,4480]{1,0:T(8,128)(2,1)S(1)} %slice.37), channel_id=1, source_target_pairs={{0,4},{2,6},{4,0},{6,2},{8,12},{10,14},{12,8},{14,10},{16,20},{18,... | collective-permute-start | bytes 3440648 | tf_op jit(solution)/shard_map/ppermute | solution.py:429
  92.9 24.1 %collective-permute-start.9 = (bf16[128,4480]{1,0:T(8,128)(2,1)}, bf16[128,4480]{1,0:T(8,128)(2,1)S(1)}, u32[]{:S(2)}, u32[]{:S(2)}) collective-permute-start(bf16[128,4480]{1,0:T(8,128)(2,1)} %slice.38), channel_id=1, source_target_pairs={{0,2},{2,0},{4,6},{6,4},{8,10},{10,8},{12,14},{14,12},{16,18},{18,... | collective-permute-start | bytes 3440648 | tf_op jit(solution)/shard_map/ppermute | solution.py:429
  126.0 51.0 %collective-permute-start.16 = (bf16[256,4096]{1,0:T(8,128)(2,1)}, bf16[256,4096]{1,0:T(8,128)(2,1)S(1)}, u32[]{:S(2)}, u32[]{:S(2)}) collective-permute-start(bf16[256,4096]{1,0:T(8,128)(2,1)} %collective-permute-done.11.refs_9_.refs_30_), channel_id=1, source_target_pairs={{0,24},{2,26},{4,28},{6,30},{8,0},{10,2},{12,4},{14,6},{16,8},{18,... | collective-permute-start | bytes 6291464 | tf_op jit(solution)/shard_map/ppermute | solution.py:440
  130.0 10.6 %collective-permute-start.12 = (bf16[144,1024]{1,0:T(8,128)(2,1)S(1)}, bf16[144,1024]{1,0:T(8,128)(2,1)S(1)}, u32[]{:S(2)}, u32[]{:S(2)}) collective-permute-start(bf16[144,1024]{1,0:T(8,128)(2,1)S(1)} %copy-done.14), channel_id=1, source_target_pairs={{0,2},{2,0},{4,6},{6,4},{8,10},{10,8},{12,14},{14,12},{16,18},{18,... | collective-permute-start | bytes 884744 | tf_op jit(solution)/shard_map/ppermute | solution.py:429
  131.2 9.4 %collective-permute-start.13 = (bf16[144,1024]{1,0:T(8,128)(2,1)S(1)}, bf16[144,1024]{1,0:T(8,128)(2,1)S(1)}, u32[]{:S(2)}, u32[]{:S(2)}) collective-permute-start(bf16[144,1024]{1,0:T(8,128)(2,1)S(1)} %copy-done.14), channel_id=1, source_target_pairs={{0,4},{2,6},{4,0},{6,2},{8,12},{10,14},{12,8},{14,10},{16,20},{18,... | collective-permute-start | bytes 884744 | tf_op jit(solution)/shard_map/ppermute | solution.py:429
  132.5 11.8 %collective-permute-start.14 = (bf16[144,1024]{1,0:T(8,128)(2,1)S(1)}, bf16[144,1024]{1,0:T(8,128)(2,1)S(1)}, u32[]{:S(2)}, u32[]{:S(2)}) collective-permute-start(bf16[144,1024]{1,0:T(8,128)(2,1)S(1)} %copy-done.14), channel_id=1, source_target_pairs={{0,6},{2,4},{4,2},{6,0},{8,14},{10,12},{12,10},{14,8},{16,22},{18,... | collective-permute-start | bytes 884744 | tf_op jit(solution)/shard_map/ppermute | solution.py:429
  167.3 5.4 %collective-permute-start.15 = (bf16[4,2,256,256]{3,2,1,0:T(8,128)(2,1)}, bf16[4,2,256,256]{3,2,1,0:T(8,128)(2,1)S(1)}, u32[]{:S(2)}, u32[]{:S(2)}) collective-permute-start(bf16[4,2,256,256]{3,2,1,0:T(8,128)(2,1)} %get-tuple-element.126), channel_id=1, source_target_pairs={{0,1},{1,0},{2,3},{3,2},{4,5},{5,4},{6,7},{7,6},{8,9},{9,8},{10,11... | collective-permute-start | bytes 3145736 | tf_op jit(solution)/shard_map/ppermute | solution.py:658
  182.8 12.8 %copy-start.19 = (f32[256,128]{1,0:T(8,128)S(1)}, f32[256,128]{1,0:T(8,128)}, u32[]{:S(2)}) copy-start(f32[256,128]{1,0:T(8,128)} %get-tuple-element.149) | copy-start | bytes 393220
  182.9 12.8 %copy-start.20 = (f32[256,128]{1,0:T(8,128)S(1)}, f32[256,128]{1,0:T(8,128)}, u32[]{:S(2)}) copy-start(f32[256,128]{1,0:T(8,128)} %get-tuple-element.150) | copy-start | bytes 393220
  182.9 21.9 %copy-start.13 = (bf16[256,128]{1,0:T(8,128)(2,1)S(1)}, bf16[256,128]{1,0:T(8,128)(2,1)}, u32[]{:S(2)}) copy-start(bf16[256,128]{1,0:T(8,128)(2,1)} %get-tuple-element.108.refs_8_.refs_2_) | copy-start | bytes 196612
  182.9 21.9 %copy-start.21 = (f32[256,128]{1,0:T(8,128)S(1)}, f32[256,128]{1,0:T(8,128)}, u32[]{:S(2)}) copy-start(f32[256,128]{1,0:T(8,128)} %get-tuple-element.151) | copy-start | bytes 393220
  182.9 22.0 %copy-start = (bf16[256,640]{1,0:T(8,128)(2,1)S(1)}, bf16[256,640]{1,0:T(8,128)(2,1)}, u32[]{:S(2)}) copy-start(bf16[256,640]{1,0:T(8,128)(2,1)} %get-tuple-element.140.refs_0_) | copy-start | bytes 983044
  182.9 22.0 %copy-start.1 = (s32[3]{0:T(128)S(1)}, s32[3]{0:T(128)}, u32[]{:S(2)}) copy-start(s32[3]{0:T(128)} %pad_add_fusion.at) | copy-start | bytes 40
  182.9 4.2 %collective-permute-start.20 = (bf16[1024,256]{1,0:T(8,128)(2,1)S(1)}, bf16[1024,256]{1,0:T(8,128)(2,1)S(1)}, u32[]{:S(2)}, u32[]{:S(2)}) collective-permute-start(bf16[1024,256]{1,0:T(8,128)(2,1)S(1)} %convolution_convert_fusion), channel_id=1, source_target_pairs={{0,1},{2,3},{4,5},{6,7},{9,8},{11,10},{13,12},{15,14},{17,16},{19,... | collective-permute-start | bytes 1572872 | tf_op jit(solution)/shard_map/ppermute | solution.py:675
  184.3 8.3 %collective-permute-start.17 = (bf16[256,640]{1,0:T(8,128)(2,1)S(1)}, bf16[256,640]{1,0:T(8,128)(2,1)S(1)}, u32[]{:S(2)}, u32[]{:S(2)}) collective-permute-start(bf16[256,640]{1,0:T(8,128)(2,1)S(1)} %copy-done.24), channel_id=1, source_target_pairs={{0,2},{2,0},{4,6},{6,4},{8,10},{10,8},{12,14},{14,12},{16,18},{18,... | collective-permute-start | bytes 983048 | tf_op jit(solution)/shard_map/ppermute | solution.py:429
  185.3 10.4 %collective-permute-start.18 = (bf16[256,640]{1,0:T(8,128)(2,1)S(1)}, bf16[256,640]{1,0:T(8,128)(2,1)S(1)}, u32[]{:S(2)}, u32[]{:S(2)}) collective-permute-start(bf16[256,640]{1,0:T(8,128)(2,1)S(1)} %copy-done.23), channel_id=1, source_target_pairs={{0,4},{2,6},{4,0},{6,2},{8,12},{10,14},{12,8},{14,10},{16,20},{18,... | collective-permute-start | bytes 983048 | tf_op jit(solution)/shard_map/ppermute | solution.py:429
  186.0 14.5 %collective-permute-start.19 = (bf16[256,640]{1,0:T(8,128)(2,1)S(1)}, bf16[256,640]{1,0:T(8,128)(2,1)S(1)}, u32[]{:S(2)}, u32[]{:S(2)}) collective-permute-start(bf16[256,640]{1,0:T(8,128)(2,1)S(1)} %copy-done.22), channel_id=1, source_target_pairs={{0,6},{2,4},{4,2},{6,0},{8,14},{10,12},{12,10},{14,8},{16,22},{18,... | collective-permute-start | bytes 983048 | tf_op jit(solution)/shard_map/ppermute | solution.py:429
  187.3 15.1 %collective-permute-start.21 = (bf16[256,256]{1,0:T(8,128)(2,1)S(1)}, bf16[256,256]{1,0:T(8,128)(2,1)S(1)}, u32[]{:S(2)}, u32[]{:S(2)}) collective-permute-start(bf16[256,256]{1,0:T(8,128)(2,1)S(1)} %get-tuple-element.154), channel_id=1, source_target_pairs={{1,3},{3,1},{5,7},{7,5},{8,10},{10,8},{12,14},{14,12},{16,18},{18,... | collective-permute-start | bytes 393224 | tf_op jit(solution)/shard_map/ppermute | solution.py:680
  190.0 13.3 %collective-permute-start.22 = (bf16[256,256]{1,0:T(8,128)(2,1)S(1)}, bf16[256,256]{1,0:T(8,128)(2,1)S(1)}, u32[]{:S(2)}, u32[]{:S(2)}) collective-permute-start(bf16[256,256]{1,0:T(8,128)(2,1)S(1)} %get-tuple-element.153), channel_id=1, source_target_pairs={{1,5},{3,7},{5,1},{7,3},{8,12},{10,14},{12,8},{14,10},{16,20},{18,... | collective-permute-start | bytes 393224 | tf_op jit(solution)/shard_map/ppermute | solution.py:680
  192.7 12.0 %collective-permute-start.23 = (bf16[256,256]{1,0:T(8,128)(2,1)S(1)}, bf16[256,256]{1,0:T(8,128)(2,1)S(1)}, u32[]{:S(2)}, u32[]{:S(2)}) collective-permute-start(bf16[256,256]{1,0:T(8,128)(2,1)S(1)} %get-tuple-element.152), channel_id=1, source_target_pairs={{1,7},{3,5},{5,3},{7,1},{8,14},{10,12},{12,10},{14,8},{16,22},{18,... | collective-permute-start | bytes 393224 | tf_op jit(solution)/shard_map/ppermute | solution.py:680
  204.8 1.8 collective-permute-start.24
  (18 other events, 70.6 us)
